TPU v7x, 256 devices: a whole 4x4x8 slice. The times are simulated.
256 devices in a mesh: rep: 4 (over y_lo, core), shard: 64 (over z, x, y_hi).
Axes of the slice: x: 4, y: 4 (y_hi: 2, y_lo: 2; y = y_hi * 2 + y_lo), z: 8, core: 2. Of those that a mesh axis runs over, the one named last changes fastest.
Arguments:
- local_weights: bfloat16 [4, 1024, 8192], P('rep', 'shard'), may hold values from -6 to 6
- base: bfloat16 [1024, 8192], P('shard'), may hold values from -6 to 6
- error: float32 [4, 1024, 8192], P('rep', 'shard'), may hold values from -4 to 4
- momentum: float32 [1024, 8192], P('shard'), may hold values from -4 to 4
- signs: int32 [8192], replicated, may hold values from -1 to 1, as said below
- kept: int32 [2, 1024], replicated, may hold values from 0 to 4095, as said below
Outputs:
- new_base: bfloat16 [1024, 8192], replicated
- new_error: float32 [4, 1024, 8192], P('rep', 'shard')
- new_momentum: float32 [1024, 8192], P('shard')
Inputs may be any that keep to these rules, and one draw needn't show every extreme that they name: `signs`: each entry is -1 or 1. `kept`: the 1024 positions of each block are distinct.
All inputs are finite; a program needn't handle non-finite values.
Results may differ from a plain program's by a relative error of at most 0.001.
Values may be sent and summed in bfloat16 or wider, within the bound.
A program may use at most 128 MiB of HBM per device.

v0:
```python
import jax
import jax.numpy as jnp
from jax import lax
from jax.sharding import PartitionSpec as P

FAC = 64


momentum_rate = 0.9
outer_rate = 0.7


def hadamard(order):
    index = jnp.arange(order, dtype=jnp.int32)
    both = jnp.bitwise_and(index[:, None], index[None, :])
    parity = jnp.zeros((order, order), jnp.int32)
    for bit in range(order.bit_length() - 1):
        parity = parity + jnp.bitwise_and(jnp.right_shift(both, bit), 1)
    return (1 - 2 * (parity % 2)).astype(jnp.float32)


def rotate(values, table):
    rows, nblk, block = values.shape
    order = table.shape[0]
    grid = values.reshape(rows, nblk, order, order)
    first = jnp.einsum("rkab,ac->rkcb", grid, table, precision=lax.Precision.HIGHEST)
    second = jnp.einsum("rkcb,bd->rkcd", first, table, precision=lax.Precision.HIGHEST)
    return second.reshape(rows, nblk, block) / order


def finish(average, base_rows, momentum_rows, table, sign_rows, blocks, kept):
    rows, nblk, block = (average.shape[0], sign_rows.shape[0], sign_rows.shape[1])
    full = jnp.zeros((rows, nblk, block), jnp.float32).at[:, blocks, kept].set(average)
    outer = (rotate(full, table) * sign_rows).reshape(rows, nblk * block)
    fresh_momentum = momentum_rate * momentum_rows + outer
    fresh_base = (
        base_rows.astype(jnp.float32) - outer_rate * (outer + momentum_rate * fresh_momentum)
    ).astype(jnp.bfloat16)
    return (fresh_base, fresh_momentum)


def shards(local_weights, base, error, momentum, signs, kept):
    rows, width = base.shape
    nblk, keep = kept.shape
    block = width // nblk
    table = hadamard(FAC)
    sign_rows = signs.astype(jnp.float32).reshape(nblk, block)
    blocks = jnp.arange(nblk, dtype=jnp.int32)[:, None]
    mask = jnp.zeros((nblk, block), jnp.float32).at[blocks, kept].set(1.0)
    compensated = base.astype(jnp.float32) - local_weights[0].astype(jnp.float32) + error[0]
    rotated = rotate(compensated.reshape(rows, nblk, block) * sign_rows, table)
    sketch = rotated[:, blocks, kept]
    dropped = (rotate(rotated * (1.0 - mask), table) * sign_rows).reshape(1, rows, width)
    replicas = lax.axis_size("rep")
    summed = lax.psum(sketch, "rep")
    fresh_base, new_momentum = finish(
        summed / replicas, base, momentum, table, sign_rows, blocks, kept
    )
    new_base = lax.all_gather(fresh_base, "shard", axis=0, tiled=True)
    return (new_base, dropped, new_momentum)


def solution(mesh):
    in_specs = (
        P("rep", "shard", None),
        P("shard", None),
        P("rep", "shard", None),
        P("shard", None),
        P(),
        P(),
    )
    out_specs = (P(), P("rep", "shard", None), P("shard", None))
    return jax.shard_map(shards, mesh=mesh, in_specs=in_specs, out_specs=out_specs, check_vma=False)
```

profile of v0, /device:TPU:1, one launch (start us, length us, event | category | flops | bytes accessed | tf_op | source)
XLA Modules:
  0.0 334.2 jit_solution(9425631497111202822)
XLA Ops:
  7.2 0.7 or_bitcast_fusion
  7.9 0.8 convert_element_type.33
  8.8 1.3 fusion.4
  10.0 0.4 reshape.63
  10.5 1.1 convolution_bitcast_fusion.2
  11.5 1.0 broadcast_multiply_fusion.1
  12.6 2.7 copy.12
  15.4 31.8 %gather_fusion = f32[2048,16]{1,0:T(8,128)} fusion(f32[16,2,4096]{0,2,1:T(8,128)} %bitcast.58, s32[2048]{0:T(1024)S(1)} %bitcast.56), kind=kCustom, calls=%fused_computation | custom fusion | bytes 278528 | tf_op jit(solution)/shard_map/gather | solution.py:52
  47.3 0.1 and_reduce_fusion
  47.5 50.5 %all-reduce.2.cloned.1.call-done = f32[16,2,1024]{0,2,1:T(8,128)} async-done(((f32[16,2,1024]{0,2,1:T(8,128)}), f32[16,2,1024]{0,2,1:T(8,128)}) %all-reduce.2.cloned.1.call-update) | async-done | bytes 131088 | tf_op jit(solution)/shard_map/psum | solution.py:55
  98.0 1.3 broadcast_multiply_fusion
  99.3 7.8 %scatter_custom_fusion = f32[16,8192]{0,1:T(8,128)} fusion(s32[2048]{0:T(1024)S(1)} %bitcast.61, f32[2048,16]{1,0:T(8,128)S(1)} %bitcast.60, f32[]{:T(128)} %constant.19.clone.1), kind=kCustom, calls=%fused_computation.3 | custom fusion | bytes 524292
  107.1 3.1 copy.11
  110.2 1.1 convolution_bitcast_fusion.1
  111.3 1.0 fusion.16
  112.3 0.4 reshape.65
  112.7 1.0 fusion.5
  113.7 8.3 %scatter_custom_fusion.1 = f32[8192]{0:T(1024)S(1)} fusion(s32[2048]{0:T(1024)S(1)} %bitcast.62, f32[2048]{0:T(1024)S(1)} %broadcast.102, f32[]{:T(128)} %constant.19.clone.1), kind=kCustom, calls=%fused_computation.35 | custom fusion | bytes 32772
  122.1 1.1 convolution_bitcast_fusion
  123.2 1.0 fusion.13
  124.2 0.4 reshape.66
  124.6 0.8 broadcast_multiply_fusion.2
  125.4 188.0 %all-gather.2.cloned.1.call-done = bf16[1024,8192]{1,0:T(8,128)(2,1)} async-done(((bf16[16,8192]{1,0:T(8,128)(2,1)}), bf16[1024,8192]{1,0:T(8,128)(2,1)}) %all-gather.2.cloned.1.call-update) | async-done | bytes 16777232 | tf_op jit(solution)/shard_map/all_gather | solution.py:59
  313.4 13.9 %copy.21 = bf16[1024,8192]{1,0:T(8,128)(2,1)} copy(bf16[1024,8192]{1,0:T(8,128)(2,1)} %all-gather.2.cloned.1.call-done) | data formatting | bytes 33554432
  (27 shorter events, 0.4 us)
Async XLA Ops:
  7.2 90.9 %all-reduce.2.cloned.1.call-start = ((), (), s32[]{:S(2)}) async-start(), calls=%async_computation | async-start | bytes 2097152 | tf_op jit(solution)/shard_map/psum | solution.py:55
  12.6 34.7 %copy-start.3 = (s32[2,1024]{1,0:T(2,128)S(1)}, s32[2,1024]{1,0:T(2,128)}, u32[]{:S(2)}) copy-start(s32[2,1024]{1,0:T(2,128)} %param.11) | copy-start | bytes 24580
  12.6 34.7 %copy-start.5 = (s32[2]{0:T(128)S(1)}, s32[2]{0:T(128)}, u32[]{:S(2)}) copy-start(s32[2]{0:T(128)} %constant.55) | copy-start | bytes 28
  12.6 34.8 %copy-start.4 = (s32[2]{0:T(128)S(1)}, s32[2]{0:T(128)}, u32[]{:S(2)}) copy-start(s32[2]{0:T(128)} %constant.52) | copy-start | bytes 28
  12.6 34.9 %copy-start.2 = (s32[8192]{0:T(1024)S(1)}, s32[8192]{0:T(1024)}, u32[]{:S(2)}) copy-start(s32[8192]{0:T(1024)} %param.10) | copy-start | bytes 98308
  47.2 266.2 %all-gather.2.cloned.1.call-start = ((), (), s32[]{:S(2)}) async-start(), calls=%async_computation.1 | async-start | bytes 17039360 | tf_op jit(solution)/shard_map/all_gather | solution.py:59
  110.2 2.5 copy-start
  110.2 2.5 copy-start.1
Sparse Core Ops, SparseCore 0:
  47.3 50.6 all-reduce.1
  113.9 199.5 all-gather.1
where the time goes:
time: 335 us; the launch traced here: 334 us
  waiting for transfers between devices  239 us (71%)
  local copies, waits for them, and re-layouts  69 us (21%)
  between operations  14.3 us (4%)
  matrix products  6.24 us (2%)
  other arithmetic  6.09 us (2%)
    all_gather x1, waiting for transfers between devices, shards(): new_base = lax.all_gather(fresh_base, 'shard', axis=0, tiled=True)  188 us
    psum x1, waiting for transfers between devices, shards(): summed = lax.psum(sketch, 'rep')  50.5 us
    gather x1, local copies, waits for them, and re-layouts, shards(): sketch = rotated[:, blocks, kept]  31.8 us
    unnamed x18, local copies, waits for them, and re-layouts  30.1 us
  transfers between devices with their start and end apart: 2, of which 2 were waited for; matrix products, arithmetic and copies ran while one was open for 4% of the time, Pallas kernels for 0%

commit v1 on v0

v1 whole, which is shorter than its diff:
```python
import functools
import heapq

import jax
import jax.numpy as jnp
from jax import lax
from jax.experimental import pallas as pl
from jax.experimental.pallas import tpu as pltpu
from jax.sharding import PartitionSpec as P

MESH = pl.DeviceIdType.MESH
SIZES = {"x": 4, "y": 4, "z": 8}
AXES = ("x", "y", "z")
ROWS, QUARTER, LANES = 16, 2048, 128
PARTS = {"A": ("xyz", 0, 5), "B": ("yzx", 5, 6), "C": ("zxy", 11, 5)}
READY = {"A": 0.0, "B": 0.6, "C": 1.2}
TILE_US, HOP_US, OP_US, LEAD_US = 0.089, 1.7, 0.03, 1.0


def ring(axis, tiles):
    half = SIZES[axis] // 2
    middle = tiles // 2
    chains = []
    for sign, first, last in ((1, 0, middle), (-1, middle, tiles)):
        chains.append((sign, [(hop, 0, tiles) for hop in range(1, half)] + [(half, first, last)]))
    return chains


def messages():
    found = {}

    def chain(part, stage, tag, axis, region, tiles, start):
        order, low, _ = PARTS[part]
        arrived = {0: start}
        for sign, hops in ring(axis, tiles):
            before = start
            for hop, first, last in hops:
                name = (part, stage) + tag + (sign, hop)
                place = dict(region)
                place[axis] = -sign * hop
                found[name] = dict(
                    part=part, stage=stage, axis=axis, sign=sign, hop=hop, region=place,
                    tiles=(low + first, low + last), after=list(before),
                )
                before = [name]
                key = -sign * hop if 2 * hop < SIZES[axis] else SIZES[axis] // 2
                arrived.setdefault(key, []).append(name)
        return arrived

    for part, (order, _, tiles) in PARTS.items():
        one, two, three = order
        own = [("own", part)]
        firsts = chain(part, 1, (), one, {one: 0, two: 0, three: 0}, tiles, own)
        seconds = {}
        for off, names in firsts.items():
            got = chain(part, 2, (off,), two, {one: off, two: 0, three: 0}, tiles, names)
            for place, news in got.items():
                if place != 0:
                    seconds.setdefault(place, []).extend(news)
        for off, names in firsts.items():
            chain(part, 3, (off, "one"), three, {one: off, two: 0, three: 0}, tiles, names)
        for off, names in seconds.items():
            chain(part, 3, (off, "all"), three, {one: None, two: off, three: 0}, tiles, names)
    return found


def count(message):
    wide = 1
    for axis, place in message["region"].items():
        wide *= SIZES[axis] if place is None else 1
    return wide * (message["tiles"][1] - message["tiles"][0])


def schedule(found):
    users = {}
    for name, message in found.items():
        for before in message["after"]:
            users.setdefault(before, []).append(name)
    needs = {name: len(message["after"]) for name, message in found.items()}
    events, queues, active, steps = [], {}, {}, []
    ticket = 0

    def push(time, rank, kind, what):
        nonlocal ticket
        ticket += 1
        heapq.heappush(events, (time, rank, ticket, kind, what))

    def kick(link, time):
        if active.get(link) or not queues.get(link):
            return
        _, _, ready, name = heapq.heappop(queues[link])
        active[link] = True
        length = count(found[name]) * TILE_US
        steps.append((max(ready, time - LEAD_US), 1, len(steps), "send", name))
        push(time + length, 1, "free", link)
        push(time + length + HOP_US, 0, "arrive", name)

    for part, time in READY.items():
        push(time, 0, "arrive", ("own", part))
    clock = 0.0
    while events:
        time, _, _, kind, what = heapq.heappop(events)
        if kind == "free":
            active[what] = False
            kick(what, time)
        elif kind == "issue":
            message = found[what]
            link = (message["axis"], message["sign"])
            ticket += 1
            heapq.heappush(queues.setdefault(link, []), (message["stage"], ticket, time, what))
            kick(link, time)
        else:
            clock = max(clock, time) + OP_US
            steps.append((clock, 0, len(steps), "wait", what))
            for name in users.get(what, []):
                needs[name] -= 1
                if needs[name] == 0:
                    clock += OP_US
                    push(clock, 0, "issue", name)
            clock += OP_US
    steps.sort()
    return [(kind, what) for _, _, _, kind, what in steps]


def forwards(found):
    groups = {}
    for name, message in found.items():
        part = message["part"]
        order, low, tiles = PARTS[part]
        one, two, three = order
        fold = lambda axis: None if message["region"][axis] is None else message["region"][axis] % SIZES[axis]
        if message["stage"] == 1:
            key = (part, 1, 0, 0)
        elif message["stage"] == 2:
            key = (part, 2, fold(two), 0)
        else:
            key = (part, 3, fold(two), fold(three))
        region = {one: None, two: key[2], three: key[3]}
        groups.setdefault(key, (region, (low, low + tiles), []))[2].append(name)
    for part in PARTS:
        groups[(part, 1, 0, 0)][2].append(("own", part))
    return list(groups.values())


def parity_table(rows, columns):
    i = lax.broadcasted_iota(jnp.int32, (rows, columns), 0)
    j = lax.broadcasted_iota(jnp.int32, (rows, columns), 1)
    both = jnp.bitwise_and(jnp.bitwise_and(i, j), LANES - 1)
    for shift in (4, 2, 1):
        both = jnp.bitwise_xor(both, jnp.right_shift(both, shift))
    return (1 - 2 * jnp.bitwise_and(both, 1)).astype(jnp.bfloat16)


def rotate(tiles, table):
    number, rows, lanes = tiles.shape
    flat = tiles.reshape(number * rows, lanes)
    high = flat.astype(jnp.bfloat16)
    low = (flat - high.astype(jnp.float32)).astype(jnp.bfloat16)
    flat = jnp.dot(jnp.concatenate([high, low], axis=1), table, preferred_element_type=jnp.float32)
    near = 1
    while near < number:
        pairs = flat.reshape(number // (2 * near), 2, near * rows, lanes)
        flat = jnp.concatenate(
            [(pairs[:, 0] + pairs[:, 1])[:, None], (pairs[:, 0] - pairs[:, 1])[:, None]], axis=1
        )
        near *= 2
    return flat.reshape(number, rows, lanes)


def sketch_kernel(lw_ref, base_ref, error_ref, signs_ref, kept_ref, kept_part_ref, dropped_ref):
    table = parity_table(2 * LANES, LANES)
    nblk, keep = kept_ref.shape
    tiles = signs_ref.shape[0] // nblk
    block = tiles * LANES
    scale = 1.0 / 64.0
    for b in range(nblk):
        columns = pl.ds(b * block, block)
        compensated = (
            base_ref[:, columns].astype(jnp.float32) - lw_ref[0, :, columns].astype(jnp.float32)
        ) + error_ref[0, :, columns]
        comp = jnp.stack([compensated[:, t * LANES:(t + 1) * LANES] for t in range(tiles)])
        signs = signs_ref[pl.ds(b * tiles, tiles), :].astype(jnp.float32)[:, None, :]
        places = kept_ref[pl.ds(b, 1), :]
        outer_hot = lax.broadcasted_iota(jnp.int32, (tiles, keep), 0) == jnp.right_shift(places, 7)
        inner_hot = lax.broadcasted_iota(jnp.int32, (LANES, keep), 0) == jnp.bitwise_and(places, LANES - 1)
        mask = lax.dot_general(
            outer_hot.astype(jnp.bfloat16), inner_hot.astype(jnp.bfloat16),
            (((1,), (1,)), ((), ())), preferred_element_type=jnp.float32,
        )[:, None, :]
        rotated = rotate(comp * signs, table) * scale
        back = rotate(jnp.where(mask > 0.5, rotated, 0.0), table) * (signs * scale)
        rest = comp - back
        half = tiles // 2
        for t in range(tiles):
            kept_part_ref[2 * b + t // half, :, pl.ds((t % half) * LANES, LANES)] = back[t]
            dropped_ref[:, pl.ds(b * block + t * LANES, LANES)] = rest[t]


def exchange_kernel(
    steps, found, joined,
    part_ref, base_ref, momentum_ref, whole_ref, fresh_ref,
    near, far, mine, outer,
    near_send, near_recv, far_send, far_recv, outer_send, outer_recv,
    stage_send, message_recv, core_send, core_recv,
):
    rep, shard = lax.axis_index("rep"), lax.axis_index("shard")
    p, c = rep // 2, rep % 2
    here = {"x": (shard // 2) % 4, "y": (shard % 2) * 2 + p, "z": shard // 8}

    def device(x, y, z, core):
        return ((y % 2) * 2 + core, z * 8 + x * 2 + y // 2)

    def moved(axis, sign):
        there = dict(here)
        there[axis] = lax.rem(here[axis] + sign + SIZES[axis], SIZES[axis])
        return device(there["x"], there["y"], there["z"], c)

    other_core = device(here["x"], here["y"], here["z"], 1 - c)
    partner = device(here["x"], (shard % 2) * 2 + 1 - p, here["z"], c)
    around = {(axis, sign): moved(axis, sign) for axis in AXES for sign in (1, -1)}

    barrier = pltpu.get_barrier_semaphore()
    for target in list(around.values()) + [other_core]:
        pl.semaphore_signal(barrier, inc=1, device_id=target, device_id_type=MESH)
    pl.semaphore_wait(barrier, 7)

    def remote(source, target, send, recv, where):
        return pltpu.make_async_remote_copy(
            src_ref=source, dst_ref=target, send_sem=send, recv_sem=recv, device_id=where, device_id_type=MESH
        )

    def at(region, tiles, core):
        index = {}
        for axis in AXES:
            place = region[axis]
            if place is None:
                index[axis] = None
            else:
                index[axis] = lax.rem(here[axis] + place + SIZES[axis], SIZES[axis])
        y_high = slice(None) if index["y"] is None else index["y"] // 2
        y_low = slice(None) if index["y"] is None else index["y"] % 2
        z = slice(None) if index["z"] is None else index["z"]
        x = slice(None) if index["x"] is None else index["x"]
        return whole_ref.at[z, x, y_high, y_low, core, :, pl.ds(tiles[0] * LANES, (tiles[1] - tiles[0]) * LANES)]

    to_far = remote(part_ref.at[2 * (1 - p) + 1 - c], near.at[0], near_send.at[0], near_recv.at[0], other_core)
    to_mine = remote(part_ref.at[2 * p + 1 - c], near.at[1], near_send.at[1], near_recv.at[1], other_core)
    to_far.start()
    to_mine.start()
    to_far.wait_recv()
    pieces = {}
    for i, (part, (_, low, tiles)) in enumerate(PARTS.items()):
        columns = pl.ds(low * LANES, tiles * LANES)
        mine[:, columns] = part_ref[2 * (1 - p) + c, :, columns] + near[0, :, columns]
        pieces[part] = remote(mine.at[:, columns], far.at[:, columns], far_send.at[i], far_recv.at[i], partner)
        pieces[part].start()
    to_mine.wait_recv()

    names = {name: i for i, name in enumerate(found)}
    sums = {(part, stage): i for i, (part, stage) in enumerate((part, stage) for part in PARTS for stage in (1, 2, 3))}

    def sent(name):
        message = found[name]
        region = dict(message["region"])
        region[message["axis"]] += message["sign"]
        source = at(region, message["tiles"], c)
        return remote(
            source, source, stage_send.at[sums[message["part"], message["stage"]]],
            message_recv.at[names[name]], around[message["axis"], message["sign"]],
        )

    def received(name):
        message = found[name]
        place = at(message["region"], message["tiles"], c)
        return remote(
            place, place, stage_send.at[sums[message["part"], message["stage"]]],
            message_recv.at[names[name]], around[message["axis"], message["sign"]],
        )

    def own(part):
        _, low, tiles = PARTS[part]
        columns = pl.ds(low * LANES, tiles * LANES)
        pieces[part].wait_recv()
        total = (part_ref[2 * p + c, :, columns] + near[1, :, columns]) + far[:, columns]
        step = total * 0.25
        outer[2 * p + c, :, columns] = step
        wide = pl.ds(pl.multiple_of((2 * p + c) * QUARTER + low * LANES, LANES), tiles * LANES)
        fresh = 0.9 * momentum_ref[:, wide] + step
        lowered = base_ref[:, wide].astype(jnp.float32) - 0.7 * (step + 0.9 * fresh)
        whole_ref[here["z"], here["x"], here["y"] // 2, p, c, :, columns] = lowered.astype(jnp.bfloat16)

    waiting = [[set(group), region, tiles] for region, tiles, group in joined]
    to_core = []
    outer_copies = []
    owned = 0
    for kind, what in steps:
        if kind == "send":
            sent(what).start()
            continue
        if what[0] == "own":
            own(what[1])
            owned += 1
            if owned == len(PARTS):
                quarter = outer.at[2 * p + c]
                outer_copies = [
                    remote(quarter, quarter, outer_send.at[0], outer_recv.at[0], partner),
                    remote(quarter, quarter, outer_send.at[1], outer_recv.at[1], other_core),
                ]
                for copy in outer_copies:
                    copy.start()
        else:
            received(what).wait_recv()
        for entry in waiting:
            entry[0].discard(what)
        for entry in [entry for entry in waiting if not entry[0]]:
            waiting.remove(entry)
            place = at(entry[1], entry[2], c)
            remote(place, place, core_send, core_recv, other_core).start()

    their = outer.at[2 * (1 - p) + c]
    remote(their, their, outer_send.at[0], outer_recv.at[0], partner).wait_recv()
    last = remote(their, their, outer_send.at[2], outer_recv.at[2], other_core)
    last.start()
    remote(outer.at[2 * p + 1 - c], outer.at[2 * p + 1 - c], outer_send.at[1], outer_recv.at[1], other_core).wait_recv()
    final = outer.at[2 * (1 - p) + 1 - c]
    remote(final, final, outer_send.at[2], outer_recv.at[2], other_core).wait_recv()
    for q in range(4):
        columns = pl.ds(q * QUARTER, QUARTER)
        fresh_ref[:, columns] = 0.9 * momentum_ref[:, columns] + outer[q]

    everything = whole_ref.at[:, :, :, :, 1 - c]
    remote(everything, everything, core_send, core_recv, other_core).wait_recv()
    everything = whole_ref.at[:, :, :, :, c]
    remote(everything, everything, core_send, core_recv, other_core).wait_send()
    for part, (order, low, tiles) in PARTS.items():
        columns = pl.ds(low * LANES, tiles * LANES)
        for stage in (1, 2, 3):
            ends = {axis: 1 for axis in AXES}
            for axis in order[:stage - 1]:
                ends[axis] = SIZES[axis]
            ends[order[stage - 1]] = SIZES[order[stage - 1]] - 1
            spans = {1: [(1, 1)], 3: [(1, 2), (1, 1)], 4: [(2, 2)]}[ends["y"]]
            for y_high, y_low in spans:
                place = whole_ref.at[
                    pl.ds(0, ends["z"]), pl.ds(0, ends["x"]), pl.ds(0, y_high), pl.ds(0, y_low), c, :, columns
                ]
                remote(
                    place, place, stage_send.at[sums[part, stage]], core_recv, other_core
                ).wait_send()
    to_far.wait_send()
    to_mine.wait_send()
    for copy in list(pieces.values()) + outer_copies + [last]:
        copy.wait_send()


def store_kernel(whole_ref, fresh_ref, dropped_ref, base_out, error_out, momentum_out, sems):
    copies = [
        pltpu.make_async_copy(fresh_ref, momentum_out, sems.at[0]),
        pltpu.make_async_copy(dropped_ref, error_out.at[0], sems.at[1]),
    ]
    for z in range(whole_ref.shape[0]):
        for low in range(2):
            for core in range(2):
                copies.append(pltpu.make_async_copy(
                    whole_ref.at[z, :, :, low, core],
                    base_out.at[z, :, :, :, pl.ds((2 * low + core) * QUARTER, QUARTER)],
                    sems.at[len(copies)],
                ))
    for copy in copies:
        copy.start()
    for copy in copies:
        copy.wait()


def shards(local_weights, base, error, momentum, signs, kept):
    rows, width = base.shape
    vmem = pl.BlockSpec(memory_space=pltpu.VMEM)
    hbm = pl.BlockSpec(memory_space=pl.ANY)
    held = lambda array: pltpu.with_memory_space_constraint(array, pltpu.VMEM)
    part, dropped = pl.pallas_call(
        sketch_kernel,
        out_shape=(pltpu.VMEM((4, rows, QUARTER), jnp.float32), pltpu.VMEM((rows, width), jnp.float32)),
        in_specs=[vmem] * 5,
        out_specs=(vmem, vmem),
        compiler_params=pltpu.CompilerParams(vmem_limit_bytes=24 << 20),
        name="sketch",
    )(local_weights, base, error, signs.reshape(width // LANES, LANES), kept)

    found = messages()
    steps, joined = schedule(found), forwards(found)
    dma = pltpu.SemaphoreType.DMA
    whole, fresh = pl.pallas_call(
        functools.partial(exchange_kernel, steps, found, joined),
        out_shape=(
            pltpu.VMEM((8, 4, 2, 2, 2, rows, QUARTER), jnp.bfloat16),
            pltpu.VMEM((rows, width), jnp.float32),
        ),
        in_specs=[vmem] * 3,
        out_specs=(vmem, vmem),
        scratch_shapes=[
            pltpu.VMEM((2, rows, QUARTER), jnp.float32),
            pltpu.VMEM((rows, QUARTER), jnp.float32),
            pltpu.VMEM((rows, QUARTER), jnp.float32),
            pltpu.VMEM((4, rows, QUARTER), jnp.float32),
            dma((2,)), dma((2,)), dma((3,)), dma((3,)), dma((3,)), dma((3,)),
            dma((9,)), dma((len(found),)), dma, dma,
        ],
        compiler_params=pltpu.CompilerParams(
            collective_id=0, has_side_effects=True, vmem_limit_bytes=16 << 20
        ),
        name="exchange",
    )(held(part), base, momentum)

    new_base, new_error, new_momentum = pl.pallas_call(
        store_kernel,
        out_shape=(
            jax.ShapeDtypeStruct((8, 4, 2, rows, width), jnp.bfloat16),
            jax.ShapeDtypeStruct((1, rows, width), jnp.float32),
            jax.ShapeDtypeStruct((rows, width), jnp.float32),
        ),
        in_specs=[vmem] * 3,
        out_specs=(hbm, hbm, hbm),
        scratch_shapes=[dma((34,))],
        compiler_params=pltpu.CompilerParams(vmem_limit_bytes=16 << 20),
        name="store",
    )(held(whole), held(fresh), held(dropped))
    return (new_base.reshape(64 * rows, width), new_error, new_momentum)


def solution(mesh):
    in_specs = (
        P("rep", "shard", None),
        P("shard", None),
        P("rep", "shard", None),
        P("shard", None),
        P(),
        P(),
    )
    out_specs = (P(), P("rep", "shard", None), P("shard", None))
    return jax.shard_map(shards, mesh=mesh, in_specs=in_specs, out_specs=out_specs, check_vma=False)
```

time: 335 us -> 75.2 us (0.22)
  waiting for transfers between devices: 239 us -> 0 us
  Pallas kernels: 0 us -> 68.8 us
  local copies, waits for them, and re-layouts: 69 us -> 5.42 us
  between operations: 14.3 us -> 0.67 us
  matrix products: 6.24 us -> 0 us
  other arithmetic: 6.09 us -> 0 us
    all_gather x1 -> x0, waiting for transfers between devices: 188 us -> none  [shards(): new_base = lax.all_gather(fresh_base, 'shard', axis=0, tiled=True)]
    pallas_call x0 -> x3, Pallas kernels: none -> 68.8 us  [the longest x1 61.3 us: shards(): pl.pallas_call(functools.partial(exchange_kernel, steps, found, joined),...]
    psum x1 -> x0, waiting for transfers between devices: 50.5 us -> none  [shards(): summed = lax.psum(sketch, 'rep')]
    gather x1 -> x0, local copies, waits for them, and re-layouts: 31.8 us -> none  [shards(): sketch = rotated[:, blocks, kept]]
    unnamed x18 -> x12, local copies, waits for them, and re-layouts: 30.1 us -> 5.42 us
    dot_general x6 -> x0, matrix products: 6.24 us -> none  [the longest x3 3.21 us: rotate(): jnp.einsum('rkab,ac->rkcb', grid, table, precision=lax.Precision.HIGHEST)]
    reshape x4 -> x0, local copies, waits for them, and re-layouts: 4.19 us -> none  [the longest x1 3.06 us: rotate(): grid = values.reshape(rows, nblk, order, order)]
  transfers between devices with their start and end apart: 2 -> 0, of which waited for: 2 -> 0; matrix products, arithmetic and copies ran while one was open for 4% -> 0% of each run, Pallas kernels for 0% -> 0%
where the time goes in v1:
time: 75.2 us; the launch traced here: 74.9 us
  Pallas kernels  68.8 us (91%)
  local copies, waits for them, and re-layouts  5.42 us (7%)
    pallas_call x1, Pallas kernels, shards(): pl.pallas_call(functools.partial(exchange_kernel, steps, found, joined),...  61.3 us
    pallas_call x1, Pallas kernels, shards(): pl.pallas_call(store_kernel, out_shape=(jax.ShapeDtypeStruct((8, 4, 2, ro...  6.41 us
    unnamed x12, local copies, waits for them, and re-layouts  5.42 us

profile of v1, /device:TPU:1, one launch (start us, length us, event | category | flops | bytes accessed | tf_op | source)
XLA Modules:
  0.0 74.9 jit_solution(13968754651929962471)
XLA Ops:
  0.6 0.0 copy-start
  0.6 0.9 %copy-done = bf16[16,8192]{1,0:T(8,128)(2,1)S(1)} copy-done((bf16[16,8192]{1,0:T(8,128)(2,1)S(1)}, bf16[16,8192]{1,0:T(8,128)(2,1)}, u32[]{:S(2)}) %copy-start) | copy-done | bytes 262168
  1.6 0.0 copy-start.1
  1.6 1.0 %copy-done.1 = f32[1,16,8192]{2,1,0:T(8,128)S(1)} copy-done((f32[1,16,8192]{2,1,0:T(8,128)S(1)}, f32[1,16,8192]{2,1,0:T(8,128)}, u32[]{:S(2)}) %copy-start.1) | copy-done | bytes 524312
  2.6 0.0 copy-start.3
  2.6 0.9 %copy-done.3 = bf16[1,16,8192]{2,1,0:T(8,128)(2,1)S(1)} copy-done((bf16[1,16,8192]{2,1,0:T(8,128)(2,1)S(1)}, bf16[1,16,8192]{2,1,0:T(8,128)(2,1)}, u32[]{:S(2)}) %copy-start.3) | copy-done | bytes 262168
  3.6 0.0 copy-start.4
  3.6 0.8 %copy-done.4 = s32[8192]{0:T(1024)S(1)} copy-done((s32[8192]{0:T(1024)S(1)}, s32[8192]{0:T(1024)}, u32[]{:S(2)}) %copy-start.4) | copy-done | bytes 32792
  4.3 0.0 copy-start.5
  4.3 0.7 copy-done.5
  5.0 1.1 %sketch.1 = (f32[4,16,2048]{2,1,0:T(8,128)S(1)}, f32[16,8192]{1,0:T(8,128)S(1)}) custom-call(bf16[1,16,8192]{2,1,0:T(8,128)(2,1)S(1)} %copy-done.3, bf16[16,8192]{1,0:T(8,128)(2,1)S(1)} %copy-done, f32[1,16,8192]{2,1,0:T(8,128)S(1)} %copy-done.1, s32[64,128]{1,0:T(8,128)S(1)} %bitcast.2, s32[2,1024]{1,0:T(2,128)S(1)} %copy-done.5), custom_call_target="tpu_custom_call" | custom-call | tf_op jit(solution)/shard_map/sketch/pallas_call | solution.py:380
  6.1 0.0 copy-start.2
  6.1 1.0 %copy-done.2 = f32[16,8192]{1,0:T(8,128)S(1)} copy-done((f32[16,8192]{1,0:T(8,128)S(1)}, f32[16,8192]{1,0:T(8,128)}, u32[]{:S(2)}) %copy-start.2) | copy-done | bytes 524312
  7.2 61.3 %exchange.1 = (bf16[8,4,2,2,2,16,2048]{6,5,4,3,2,1,0:T(8,128)(2,1)S(1)}, f32[16,8192]{1,0:T(8,128)S(1)}) custom-call(f32[4,16,2048]{2,1,0:T(8,128)S(1)} %get-tuple-element.10.part_ref, bf16[16,8192]{1,0:T(8,128)(2,1)S(1)} %copy-done, f32[16,8192]{1,0:T(8,128)S(1)} %copy-done.2), custom_call_target="tpu_custom_call" | custom-call | tf_op jit(solution)/shard_map/exchange/pallas_call | solution.py:392
  68.5 6.4 %store.1 = (bf16[8,4,2,16,8192]{4,3,2,1,0:T(8,128)(2,1)}, f32[1,16,8192]{2,1,0:T(8,128)}, f32[16,8192]{1,0:T(8,128)}) custom-call(bf16[8,4,2,2,2,16,2048]{6,5,4,3,2,1,0:T(8,128)(2,1)S(1)} %get-tuple-element.11.whole_ref, f32[16,8192]{1,0:T(8,128)S(1)} %get-tuple-element.12.fresh_ref, f32[16,8192]{1,0:T(8,128)S(1)} %get-tuple-element.13.dropped_ref), custom_call_target="tpu_custom_call" | custom-call | tf_op jit(solution)/shard_map/store/pallas_call | solution.py:414
Async XLA Ops:
  0.6 1.0 %copy-start = (bf16[16,8192]{1,0:T(8,128)(2,1)S(1)}, bf16[16,8192]{1,0:T(8,128)(2,1)}, u32[]{:S(2)}) copy-start(bf16[16,8192]{1,0:T(8,128)(2,1)} %base_ref.3) | copy-start | bytes 786436
  1.6 1.0 %copy-start.1 = (f32[1,16,8192]{2,1,0:T(8,128)S(1)}, f32[1,16,8192]{2,1,0:T(8,128)}, u32[]{:S(2)}) copy-start(f32[1,16,8192]{2,1,0:T(8,128)} %error_ref.1) | copy-start | bytes 1572868
  2.6 0.9 %copy-start.3 = (bf16[1,16,8192]{2,1,0:T(8,128)(2,1)S(1)}, bf16[1,16,8192]{2,1,0:T(8,128)(2,1)}, u32[]{:S(2)}) copy-start(bf16[1,16,8192]{2,1,0:T(8,128)(2,1)} %lw_ref.1) | copy-start | bytes 786436
  3.6 0.8 %copy-start.4 = (s32[8192]{0:T(1024)S(1)}, s32[8192]{0:T(1024)}, u32[]{:S(2)}) copy-start(s32[8192]{0:T(1024)} %param.10) | copy-start | bytes 98308
  4.3 0.7 copy-start.5
  6.1 1.0 %copy-start.2 = (f32[16,8192]{1,0:T(8,128)S(1)}, f32[16,8192]{1,0:T(8,128)}, u32[]{:S(2)}) copy-start(f32[16,8192]{1,0:T(8,128)} %momentum_ref.1) | copy-start | bytes 1572868

commit v2 on v0

v2 whole, which is shorter than its diff:
```python
import functools
import heapq

import jax
import jax.numpy as jnp
from jax import lax
from jax.experimental import pallas as pl
from jax.experimental.pallas import tpu as pltpu
from jax.sharding import PartitionSpec as P

MESH = pl.DeviceIdType.MESH
SIZES = {"x": 4, "y": 4, "z": 8}
AXES = ("x", "y", "z")
ROWS, QUARTER, LANES = 16, 2048, 128
PARTS = {"A": ("xyz", 0, 4), "B": ("yzx", 4, 6), "C": ("zxy", 10, 6)}
STRAIGHT = {("A", 1): (2,), ("B", 1): (2,), ("C", 1): (3,)}
CUT = {("C", 3): 3}
READY = {"A": 0.0, "B": 0.9, "C": 1.6}
TILE_US, HOP_US, FAR_US, OP_US, LEAD_US = 0.089, 2.5, 0.65, 0.04, 0.8
OUTER = ("outer",)
OUTER_TILES = 32
FINISH_AFTER = 40


def messages():
    found = {}

    def chain(part, stage, tag, axis, region, start):
        _, low, tiles = PARTS[part]
        straight = STRAIGHT.get((part, stage), ())
        arrived = {0: start}
        base = (part, stage) + tag

        def add(name, step, far, place, first, last, after):
            spot = dict(region)
            spot[axis] = place
            found[base + name] = dict(
                part=part, stage=stage, link=(axis, step), far=far, region=spot,
                tiles=(low + first, low + last), after=list(after),
            )
            arrived.setdefault(place, []).append(base + name)
            return [base + name]

        if SIZES[axis] == 4:
            near = {step: add((step, 1), step, 1, step, 0, tiles, start) for step in (1, 3)}
            if 2 in straight:
                add((2, 2), 2, 2, 2, 0, tiles, start)
            else:
                cut = CUT.get((part, stage), tiles // 2)
                add((3, 2), 3, 1, 2, 0, cut, near[1])
                add((1, 2), 1, 1, 2, cut, tiles, near[3])
            return arrived
        half = SIZES[axis] // 2
        for sign, first, last in ((1, 0, tiles // 2), (-1, tiles // 2, tiles)):
            behind = {0: start}
            for hop in range(1, half + 1):
                back = 0 if hop in straight else hop - 1
                span = (0, tiles) if hop < half else (first, last)
                place = -sign * hop if hop < half else half
                behind[hop] = add((sign, hop), sign * (hop - back), hop - back, place, *span, behind[back])
        return arrived

    for part, (order, _, _) in PARTS.items():
        one, two, three = order
        firsts = chain(part, 1, (), one, {one: 0, two: 0, three: 0}, [("own", part)])
        seconds = {}
        for off, names in firsts.items():
            for place, news in chain(part, 2, (off,), two, {one: off, two: 0, three: 0}, names).items():
                if place != 0:
                    seconds.setdefault(place, []).extend(news)
        for off, names in firsts.items():
            chain(part, 3, (off, "one"), three, {one: off, two: 0, three: 0}, names)
        for off, names in seconds.items():
            chain(part, 3, (off, "all"), three, {one: None, two: off, three: 0}, names)
    found[OUTER] = dict(
        part=None, stage=4, link=("y", 1), far=1, region={}, tiles=(0, OUTER_TILES),
        after=[("own", part) for part in PARTS],
    )
    return found


def count(message):
    wide = 1
    for axis, place in message["region"].items():
        wide *= SIZES[axis] if place is None else 1
    return wide * (message["tiles"][1] - message["tiles"][0])


def forwards(found):
    groups = {}
    for name, message in found.items():
        part, stage, region = message["part"], message["stage"], message["region"]
        if part is None:
            continue
        order, low, tiles = PARTS[part]
        one, two, three = order
        key = (part, stage, region[two] if stage > 1 else 0, region[three] if stage > 2 else 0)
        groups.setdefault(key, ({one: None, two: key[2], three: key[3]}, (low, low + tiles), []))[2].append(name)
    for part in PARTS:
        groups[(part, 1, 0, 0)][2].append(("own", part))
    return list(groups.values())


def schedule(found, joined):
    users = {}
    for name, message in found.items():
        for before in message["after"]:
            users.setdefault(before, []).append(name)
    length = {name: count(message) * TILE_US for name, message in found.items()}
    delay = {name: HOP_US + FAR_US * (message["far"] - 1) for name, message in found.items()}
    remaining = {}

    def path(name):
        if name not in remaining:
            remaining[name] = length[name] + delay[name] + max([path(user) for user in users.get(name, [])] + [0.0])
        return remaining[name]

    def lanes(link):
        axis, step = link
        if axis == "z":
            return [((axis, 1 if step > 0 else -1), abs(step))]
        return [((axis, 1), 1), ((axis, 3), 1)] if step == 2 else [(link, 1)]

    needs = {name: len(message["after"]) for name, message in found.items()}
    cores = [set(names) for _, _, names in joined]
    arrivals = [(time, -1, ("own", part)) for part, time in READY.items()]
    heapq.heapify(arrivals)
    queues, free, steps = {}, {}, []
    clock, ticket = 0.0, 0
    while arrivals or any(queues.values()):
        if arrivals and arrivals[0][0] <= clock:
            what = heapq.heappop(arrivals)[2]
            clock += OP_US
            steps.append(("wait", what))
            for user in users.get(what, []):
                needs[user] -= 1
                if needs[user] == 0:
                    ticket += 1
                    heapq.heappush(queues.setdefault(found[user]["link"], []), (-path(user), ticket, user))
            for names in cores:
                names.discard(what)
            clock += OP_US * sum(1 for names in cores if not names)
            cores = [names for names in cores if names]
            continue
        backlog = {
            link: max(free.get(lane, 0.0) for lane, _ in lanes(link)) for link, queue in queues.items() if queue
        }
        open_links = [(max(until - clock, 0.0), link) for link, until in backlog.items() if until - clock < LEAD_US]
        if open_links:
            _, _, name = heapq.heappop(queues[min(open_links)[1]])
            clock += OP_US
            steps.append(("send", name))
            end = 0.0
            for lane, times in lanes(found[name]["link"]):
                free[lane] = max(clock, free.get(lane, 0.0)) + length[name] * times
                end = max(end, free[lane])
            ticket += 1
            heapq.heappush(arrivals, (end + delay[name], ticket, name))
            continue
        later = [until - LEAD_US + 1e-6 for until in backlog.values()]
        if arrivals:
            later.append(arrivals[0][0])
        clock = max(clock, min(later))
    return steps


def parity_table(rows, columns):
    i = lax.broadcasted_iota(jnp.int32, (rows, columns), 0)
    j = lax.broadcasted_iota(jnp.int32, (rows, columns), 1)
    both = jnp.bitwise_and(jnp.bitwise_and(i, j), LANES - 1)
    for shift in (4, 2, 1):
        both = jnp.bitwise_xor(both, jnp.right_shift(both, shift))
    return (1 - 2 * jnp.bitwise_and(both, 1)).astype(jnp.bfloat16)


def rotate(tiles, table):
    number, rows, lanes = tiles.shape
    flat = tiles.reshape(number * rows, lanes)
    high = flat.astype(jnp.bfloat16)
    low = (flat - high.astype(jnp.float32)).astype(jnp.bfloat16)
    flat = jnp.dot(jnp.concatenate([high, low], axis=1), table, preferred_element_type=jnp.float32)
    near = 1
    while near < number:
        pairs = flat.reshape(number // (2 * near), 2, near * rows, lanes)
        flat = jnp.concatenate(
            [(pairs[:, 0] + pairs[:, 1])[:, None], (pairs[:, 0] - pairs[:, 1])[:, None]], axis=1
        )
        near *= 2
    return flat.reshape(number, rows, lanes)


def exchange_kernel(
    steps, found, joined,
    lw_ref, base_ref, error_ref, momentum_ref, signs_ref, kept_ref,
    whole_ref, fresh_ref, dropped_ref,
    lw, base, error, momentum, signs, kept, part_sums, near, far, mine, outer,
    loads, near_send, near_recv, far_send, far_recv, outer_send, outer_recv,
    stage_send, message_recv, core_send, core_recv,
):
    rep, shard = lax.axis_index("rep"), lax.axis_index("shard")
    p, c = rep // 2, rep % 2
    x, y_high, z = (shard // 2) % 4, shard % 2, shard // 8
    block = base.shape[2]
    tiles_of_block = block // LANES

    def place_x(bits):
        return {0: x, 1: x + 1 - 2 * (x % 2), 2: (x + 2) % 4, 3: 3 - x}[bits]

    def place_y(bits):
        return (y_high if bits < 2 else 1 - y_high, p if bits % 2 == 0 else 1 - p)

    def place_z(step):
        return (z + step + SIZES["z"]) % SIZES["z"]

    def device(x_bits, y_bits, z_step, core):
        high, low = place_y(y_bits)
        return (low * 2 + core, place_z(z_step) * 8 + place_x(x_bits) * 2 + high)

    other_core = device(0, 0, 0, 1 - c)
    partner = device(0, 1, 0, c)

    def over(link):
        axis, step = link
        return device(step if axis == "x" else 0, step if axis == "y" else 0, step if axis == "z" else 0, c)

    copies = [pltpu.make_async_copy(signs_ref, signs, loads.at[0]), pltpu.make_async_copy(kept_ref, kept, loads.at[1])]
    for slot, b in enumerate((1 - p, p)):
        columns = pl.ds(pl.multiple_of(b * block, block), block)
        copies += [
            pltpu.make_async_copy(lw_ref.at[0, :, columns], lw.at[slot], loads.at[2 + 3 * slot]),
            pltpu.make_async_copy(base_ref.at[:, columns], base.at[slot], loads.at[3 + 3 * slot]),
            pltpu.make_async_copy(error_ref.at[0, :, columns], error.at[slot], loads.at[4 + 3 * slot]),
        ]
    copies.append(pltpu.make_async_copy(momentum_ref, momentum, loads.at[8]))
    for copy in copies:
        copy.start()

    barrier = pltpu.get_barrier_semaphore()
    peers = [over(link) for link in sorted({message["link"] for message in found.values()})] + [other_core]
    for target in peers:
        pl.semaphore_signal(barrier, inc=1, device_id=target, device_id_type=MESH)

    table = parity_table(2 * LANES, LANES)
    scale = 1.0 / 64.0

    def sketch(slot, b):
        for copy in copies[2 + 3 * slot:5 + 3 * slot]:
            copy.wait()
        compensated = (base[slot].astype(jnp.float32) - lw[slot].astype(jnp.float32)) + error[slot]
        comp = jnp.stack([compensated[:, t * LANES:(t + 1) * LANES] for t in range(tiles_of_block)])
        rows = pl.ds(pl.multiple_of(b * tiles_of_block, tiles_of_block), tiles_of_block)
        turn = signs[rows, :].astype(jnp.float32)[:, None, :]
        places = kept[pl.ds(b, 1), :]
        tile_hot = lax.broadcasted_iota(jnp.int32, (tiles_of_block, places.shape[1]), 0) == jnp.right_shift(places, 7)
        lane_hot = lax.broadcasted_iota(jnp.int32, (LANES, places.shape[1]), 0) == jnp.bitwise_and(places, LANES - 1)
        mask = lax.dot_general(
            tile_hot.astype(jnp.bfloat16), lane_hot.astype(jnp.bfloat16),
            (((1,), (1,)), ((), ())), preferred_element_type=jnp.float32,
        )[:, None, :]
        rotated = rotate(comp * turn, table) * scale
        back = rotate(jnp.where(mask > 0.5, rotated, 0.0), table) * (turn * scale)
        rest = comp - back
        half = tiles_of_block // 2
        for t in range(tiles_of_block):
            part_sums[2 * b + t // half, :, pl.ds((t % half) * LANES, LANES)] = back[t]
            dropped_ref[:, pl.ds(pl.multiple_of(b * block + t * LANES, LANES), LANES)] = rest[t]

    def remote(source, target, send, recv, where):
        return pltpu.make_async_remote_copy(
            src_ref=source, dst_ref=target, send_sem=send, recv_sem=recv, device_id=where, device_id_type=MESH
        )

    def at(region, tiles):
        every = slice(None)
        spot_x = every if region["x"] is None else place_x(region["x"])
        high, low = (every, every) if region["y"] is None else place_y(region["y"])
        spot_z = every if region["z"] is None else place_z(region["z"])
        return whole_ref.at[spot_z, spot_x, high, low, c, :, pl.ds(tiles[0] * LANES, (tiles[1] - tiles[0]) * LANES)]

    to_far = remote(part_sums.at[2 * (1 - p) + 1 - c], near.at[0], near_send.at[0], near_recv.at[0], other_core)
    to_mine = remote(part_sums.at[2 * p + 1 - c], near.at[1], near_send.at[1], near_recv.at[1], other_core)
    copies[0].wait()
    copies[1].wait()
    sketch(0, 1 - p)
    pl.semaphore_wait(barrier, len(peers))
    to_far.start()
    sketch(1, p)
    to_mine.start()
    to_far.wait_recv()
    pieces = {}
    for i, (part, (_, low, tiles)) in enumerate(PARTS.items()):
        columns = pl.ds(low * LANES, tiles * LANES)
        mine[:, columns] = part_sums[2 * (1 - p) + c, :, columns] + near[0, :, columns]
        pieces[part] = remote(mine.at[:, columns], far.at[:, columns], far_send.at[i], far_recv.at[i], partner)
        pieces[part].start()
    to_mine.wait_recv()
    copies[8].wait()

    names = {name: i for i, name in enumerate(name for name in found if name != OUTER)}
    sums = {(part, stage): 3 * i + stage - 1 for i, part in enumerate(PARTS) for stage in (1, 2, 3)}
    mine_outer, their_outer = outer.at[2 * p + c], outer.at[2 * (1 - p) + c]
    outer_far = remote(mine_outer, mine_outer, outer_send.at[0], outer_recv.at[0], partner)
    outer_near = remote(mine_outer, mine_outer, outer_send.at[1], outer_recv.at[1], other_core)
    outer_last = remote(their_outer, their_outer, outer_send.at[2], outer_recv.at[2], other_core)

    def moved(name, sender):
        message = found[name]
        axis, step = message["link"]
        region = dict(message["region"])
        if sender:
            region[axis] = region[axis] + step if axis == "z" else region[axis] ^ step
        place = at(region, message["tiles"])
        return remote(
            place, place, stage_send.at[sums[message["part"], message["stage"]]],
            message_recv.at[names[name]], over(message["link"]),
        )

    def own(part):
        _, low, tiles = PARTS[part]
        columns = pl.ds(low * LANES, tiles * LANES)
        pieces[part].wait_recv()
        total = (part_sums[2 * p + c, :, columns] + near[1, :, columns]) + far[:, columns]
        step = total * 0.25
        outer[2 * p + c, :, columns] = step
        wide = pl.ds(pl.multiple_of((2 * p + c) * QUARTER + low * LANES, LANES), tiles * LANES)
        fresh = 0.9 * momentum[:, wide] + step
        held = pl.ds(pl.multiple_of(c * QUARTER + low * LANES, LANES), tiles * LANES)
        lowered = base[1, :, held].astype(jnp.float32) - 0.7 * (step + 0.9 * fresh)
        whole_ref[z, x, y_high, p, c, :, columns] = lowered.astype(jnp.bfloat16)

    def finish():
        from_core = outer.at[2 * p + 1 - c]
        remote(from_core, from_core, outer_send.at[1], outer_recv.at[1], other_core).wait_recv()
        from_core = outer.at[2 * (1 - p) + 1 - c]
        remote(from_core, from_core, outer_send.at[2], outer_recv.at[2], other_core).wait_recv()
        for q in range(4):
            columns = pl.ds(q * QUARTER, QUARTER)
            fresh_ref[:, columns] = 0.9 * momentum[:, columns] + outer[q]

    waiting = [(set(group), region, tiles) for region, tiles, group in joined]
    outer_at = steps.index(("wait", OUTER))
    for i, (kind, what) in enumerate(steps):
        if i == outer_at + FINISH_AFTER:
            finish()
        if kind == "send":
            if what == OUTER:
                outer_far.start()
                outer_near.start()
            else:
                moved(what, True).start()
            continue
        if what == OUTER:
            remote(their_outer, their_outer, outer_send.at[0], outer_recv.at[0], partner).wait_recv()
            outer_last.start()
            continue
        if what[0] == "own":
            own(what[1])
        else:
            moved(what, False).wait_recv()
        for group, _, _ in waiting:
            group.discard(what)
        for _, region, tiles in [entry for entry in waiting if not entry[0]]:
            place = at(region, tiles)
            remote(place, place, core_send, core_recv, other_core).start()
        waiting = [entry for entry in waiting if entry[0]]
    if outer_at + FINISH_AFTER >= len(steps):
        finish()

    everything = whole_ref.at[:, :, :, :, 1 - c]
    remote(everything, everything, core_send, core_recv, other_core).wait_recv()
    everything = whole_ref.at[:, :, :, :, c]
    remote(everything, everything, core_send, core_recv, other_core).wait_send()
    for part, (order, low, tiles) in PARTS.items():
        columns = pl.ds(low * LANES, tiles * LANES)
        for stage in (1, 2, 3):
            ends = {axis: 1 for axis in AXES}
            for axis in order[:stage - 1]:
                ends[axis] = SIZES[axis]
            ends[order[stage - 1]] = SIZES[order[stage - 1]] - 1
            for high, low_y in {1: [(1, 1)], 3: [(1, 2), (1, 1)], 4: [(2, 2)]}[ends["y"]]:
                place = whole_ref.at[
                    pl.ds(0, ends["z"]), pl.ds(0, ends["x"]), pl.ds(0, high), pl.ds(0, low_y), c, :, columns
                ]
                remote(place, place, stage_send.at[sums[part, stage]], core_recv, other_core).wait_send()
    to_far.wait_send()
    to_mine.wait_send()
    for copy in list(pieces.values()) + [outer_far, outer_near, outer_last]:
        copy.wait_send()


def store_kernel(whole_ref, fresh_ref, dropped_ref, base_out, error_out, momentum_out, sems):
    copies = [
        pltpu.make_async_copy(fresh_ref, momentum_out, sems.at[0]),
        pltpu.make_async_copy(dropped_ref, error_out.at[0], sems.at[1]),
    ]
    for z in range(whole_ref.shape[0]):
        for low in range(2):
            for core in range(2):
                copies.append(pltpu.make_async_copy(
                    whole_ref.at[z, :, :, low, core],
                    base_out.at[z, :, :, :, pl.ds((2 * low + core) * QUARTER, QUARTER)],
                    sems.at[len(copies)],
                ))
    for copy in copies:
        copy.start()
    for copy in copies:
        copy.wait()


def shards(local_weights, base, error, momentum, signs, kept):
    rows, width = base.shape
    vmem = pl.BlockSpec(memory_space=pltpu.VMEM)
    hbm = pl.BlockSpec(memory_space=pl.ANY)
    held = lambda array: pltpu.with_memory_space_constraint(array, pltpu.VMEM)
    stay = lambda array: pltpu.with_memory_space_constraint(array, pltpu.HBM)
    found = messages()
    joined = forwards(found)
    steps = schedule(found, joined)
    dma = pltpu.SemaphoreType.DMA
    whole, fresh, dropped = pl.pallas_call(
        functools.partial(exchange_kernel, steps, found, joined),
        out_shape=(
            pltpu.VMEM((8, 4, 2, 2, 2, rows, QUARTER), jnp.bfloat16),
            pltpu.VMEM((rows, width), jnp.float32),
            pltpu.VMEM((rows, width), jnp.float32),
        ),
        in_specs=[hbm] * 6,
        out_specs=(vmem, vmem, vmem),
        scratch_shapes=[
            pltpu.VMEM((2, rows, width // 2), jnp.bfloat16),
            pltpu.VMEM((2, rows, width // 2), jnp.bfloat16),
            pltpu.VMEM((2, rows, width // 2), jnp.float32),
            pltpu.VMEM((rows, width), jnp.float32),
            pltpu.VMEM((width // LANES, LANES), jnp.int32),
            pltpu.VMEM(kept.shape, jnp.int32),
            pltpu.VMEM((4, rows, QUARTER), jnp.float32),
            pltpu.VMEM((2, rows, QUARTER), jnp.float32),
            pltpu.VMEM((rows, QUARTER), jnp.float32),
            pltpu.VMEM((rows, QUARTER), jnp.float32),
            pltpu.VMEM((4, rows, QUARTER), jnp.float32),
            dma((9,)), dma((2,)), dma((2,)), dma((3,)), dma((3,)), dma((3,)), dma((3,)),
            dma((9,)), dma((len(found) - 1,)), dma, dma,
        ],
        compiler_params=pltpu.CompilerParams(
            collective_id=0, has_side_effects=True, vmem_limit_bytes=16 << 20
        ),
        name="exchange",
    )(
        stay(local_weights), stay(base), stay(error), stay(momentum),
        stay(signs.reshape(width // LANES, LANES)), stay(kept),
    )

    new_base, new_error, new_momentum = pl.pallas_call(
        store_kernel,
        out_shape=(
            jax.ShapeDtypeStruct((8, 4, 2, rows, width), jnp.bfloat16),
            jax.ShapeDtypeStruct((1, rows, width), jnp.float32),
            jax.ShapeDtypeStruct((rows, width), jnp.float32),
        ),
        in_specs=[vmem] * 3,
        out_specs=(hbm, hbm, hbm),
        scratch_shapes=[dma((34,))],
        compiler_params=pltpu.CompilerParams(vmem_limit_bytes=16 << 20),
        name="store",
    )(held(whole), held(fresh), held(dropped))
    return (new_base.reshape(64 * rows, width), new_error, new_momentum)


def solution(mesh):
    in_specs = (
        P("rep", "shard", None),
        P("shard", None),
        P("rep", "shard", None),
        P("shard", None),
        P(),
        P(),
    )
    out_specs = (P(), P("rep", "shard", None), P("shard", None))
    return jax.shard_map(shards, mesh=mesh, in_specs=in_specs, out_specs=out_specs, check_vma=False)
```

time: 335 us -> 64.5 us (0.19)
  waiting for transfers between devices: 239 us -> 0 us
  local copies, waits for them, and re-layouts: 69 us -> 0 us
  Pallas kernels: 0 us -> 63.8 us
  between operations: 14.3 us -> 0.64 us
  matrix products: 6.24 us -> 0 us
  other arithmetic: 6.09 us -> 0 us
    all_gather x1 -> x0, waiting for transfers between devices: 188 us -> none  [shards(): new_base = lax.all_gather(fresh_base, 'shard', axis=0, tiled=True)]
    pallas_call x0 -> x2, Pallas kernels: none -> 63.8 us  [the longest x1 57.4 us: shards(): pl.pallas_call(functools.partial(exchange_kernel, steps, found, joined),...]
    psum x1 -> x0, waiting for transfers between devices: 50.5 us -> none  [shards(): summed = lax.psum(sketch, 'rep')]
    gather x1 -> x0, local copies, waits for them, and re-layouts: 31.8 us -> none  [shards(): sketch = rotated[:, blocks, kept]]
    unnamed x18 -> x0, local copies, waits for them, and re-layouts: 30.1 us -> none
    dot_general x6 -> x0, matrix products: 6.24 us -> none  [the longest x3 3.21 us: rotate(): jnp.einsum('rkab,ac->rkcb', grid, table, precision=lax.Precision.HIGHEST)]
    reshape x4 -> x0, local copies, waits for them, and re-layouts: 4.19 us -> none  [the longest x1 3.06 us: rotate(): grid = values.reshape(rows, nblk, order, order)]
  transfers between devices with their start and end apart: 2 -> 0, of which waited for: 2 -> 0; matrix products, arithmetic and copies ran while one was open for 4% -> 0% of each run, Pallas kernels for 0% -> 0%
where the time goes in v2:
time: 64.5 us; the launch traced here: 64.4 us
  Pallas kernels  63.8 us (99%)
    pallas_call x1, Pallas kernels, shards(): pl.pallas_call(functools.partial(exchange_kernel, steps, found, joined),...  57.4 us
    pallas_call x1, Pallas kernels, shards(): pl.pallas_call(store_kernel, out_shape=(jax.ShapeDtypeStruct((8, 4, 2, ro...  6.41 us

profile of v2, /device:TPU:1, one launch (start us, length us, event | category | flops | bytes accessed | tf_op | source)
XLA Modules:
  0.0 64.4 jit_solution(10094709753887105082)
XLA Ops:
  0.6 57.4 %exchange.1 = (bf16[8,4,2,2,2,16,2048]{6,5,4,3,2,1,0:T(8,128)(2,1)S(1)}, f32[16,8192]{1,0:T(8,128)S(1)}, f32[16,8192]{1,0:T(8,128)S(1)}) custom-call(bf16[1,16,8192]{2,1,0:T(8,128)(2,1)} %lw_ref.1, bf16[16,8192]{1,0:T(8,128)(2,1)} %base_ref.1, f32[1,16,8192]{2,1,0:T(8,128)} %error_ref.1, f32[16,8192]{1,0:T(8,128)} %momentum_ref.1, s32[64,128]{1,0:T(8,128)} %bitcast.2, ...), custom_call_target="tpu_custom_call" | custom-call | tf_op jit(solution)/shard_map/exchange/pallas_call | solution.py:420
  58.0 6.4 %store.1 = (bf16[8,4,2,16,8192]{4,3,2,1,0:T(8,128)(2,1)}, f32[1,16,8192]{2,1,0:T(8,128)}, f32[16,8192]{1,0:T(8,128)}) custom-call(bf16[8,4,2,2,2,16,2048]{6,5,4,3,2,1,0:T(8,128)(2,1)S(1)} %get-tuple-element.9.whole_ref, f32[16,8192]{1,0:T(8,128)S(1)} %get-tuple-element.10.fresh_ref, f32[16,8192]{1,0:T(8,128)S(1)} %get-tuple-element.11.dropped_ref), custom_call_target="tpu_custom_call" | custom-call | tf_op jit(solution)/shard_map/store/pallas_call | solution.py:453

commit v3 on v2

--- a/solution.py
+++ b/solution.py
@@ -15,31 +15,42 @@
 PARTS = {"A": ("xyz", 0, 4), "B": ("yzx", 4, 6), "C": ("zxy", 10, 6)}
 STRAIGHT = {("A", 1): (2,), ("B", 1): (2,), ("C", 1): (3,)}
 CUT = {("C", 3): 3}
+SINGLES = {"A": (1, 1), "B": (1, 1), "C": (1, 1)}
 READY = {"A": 0.0, "B": 0.9, "C": 1.6}
-TILE_US, HOP_US, FAR_US, OP_US, LEAD_US = 0.089, 2.5, 0.65, 0.04, 0.8
+TILE_US, HOP_US, FAR_US, OP_US, LEAD_US = 0.092, 3.1, 0.65, 0.01, 0.4
 OUTER = ("outer",)
 OUTER_TILES = 32
 FINISH_AFTER = 40
 
 
 def messages():
-    found = {}
+    found, units = {}, {}
 
     def chain(part, stage, tag, axis, region, start):
         _, low, tiles = PARTS[part]
         straight = STRAIGHT.get((part, stage), ())
         arrived = {0: start}
         base = (part, stage) + tag
+        half = SIZES[axis] // 2
 
         def add(name, step, far, place, first, last, after):
             spot = dict(region)
             spot[axis] = place
+            unit = base + name
+            whole = dict(spot)
+            if place == half:
+                unit = base + ("opposite",)
+                if stage == 3 and tag[-1] == "one":
+                    unit = (part, stage, "one", "opposite")
+                    whole[PARTS[part][0][0]] = (0, 1)
             found[base + name] = dict(
                 part=part, stage=stage, link=(axis, step), far=far, region=spot,
-                tiles=(low + first, low + last), after=list(after),
+                tiles=(low + first, low + last), after=list(after), unit=unit,
             )
-            arrived.setdefault(place, []).append(base + name)
-            return [base + name]
+            units.setdefault(unit, (whole, (low, low + tiles), []))[2].append(base + name)
+            if unit not in arrived.setdefault(place, []):
+                arrived[place].append(unit)
+            return [unit]
 
         if SIZES[axis] == 4:
             near = {step: add((step, 1), step, 1, step, 0, tiles, start) for step in (1, 3)}
@@ -50,7 +61,6 @@
                 add((3, 2), 3, 1, 2, 0, cut, near[1])
                 add((1, 2), 1, 1, 2, cut, tiles, near[3])
             return arrived
-        half = SIZES[axis] // 2
         for sign, first, last in ((1, 0, tiles // 2), (-1, tiles // 2, tiles)):
             behind = {0: start}
             for hop in range(1, half + 1):
@@ -63,56 +73,61 @@
     for part, (order, _, _) in PARTS.items():
         one, two, three = order
         firsts = chain(part, 1, (), one, {one: 0, two: 0, three: 0}, [("own", part)])
+        singles = [(off, {one: off, two: 0, three: 0}, names) for off, names in firsts.items()]
+        together = [(9, {one: (0, 1), two: 0, three: 0}, [name for names in firsts.values() for name in names])]
         seconds = {}
-        for off, names in firsts.items():
-            for place, news in chain(part, 2, (off,), two, {one: off, two: 0, three: 0}, names).items():
+        for off, region, names in singles if SINGLES[part][0] else together:
+            for place, news in chain(part, 2, (off,), two, region, names).items():
                 if place != 0:
                     seconds.setdefault(place, []).extend(news)
-        for off, names in firsts.items():
-            chain(part, 3, (off, "one"), three, {one: off, two: 0, three: 0}, names)
+        for off, region, names in singles if SINGLES[part][1] else together:
+            chain(part, 3, (off, "one"), three, region, names)
         for off, names in seconds.items():
-            chain(part, 3, (off, "all"), three, {one: None, two: off, three: 0}, names)
+            chain(part, 3, (off, "all"), three, {one: (0, 1), two: off, three: 0}, names)
     found[OUTER] = dict(
         part=None, stage=4, link=("y", 1), far=1, region={}, tiles=(0, OUTER_TILES),
-        after=[("own", part) for part in PARTS],
+        after=[("own", part) for part in PARTS], unit=OUTER,
     )
-    return found
-
-
-def count(message):
+    units[OUTER] = ({}, None, [OUTER])
+    return found, units
+
+
+def count(region, tiles):
     wide = 1
-    for axis, place in message["region"].items():
-        wide *= SIZES[axis] if place is None else 1
-    return wide * (message["tiles"][1] - message["tiles"][0])
+    for axis, place in region.items():
+        wide *= SIZES[axis] if isinstance(place, tuple) else 1
+    return wide * (tiles[1] - tiles[0])
 
 
 def forwards(found):
     groups = {}
-    for name, message in found.items():
+    for message in found.values():
         part, stage, region = message["part"], message["stage"], message["region"]
         if part is None:
             continue
         order, low, tiles = PARTS[part]
         one, two, three = order
         key = (part, stage, region[two] if stage > 1 else 0, region[three] if stage > 2 else 0)
-        groups.setdefault(key, ({one: None, two: key[2], three: key[3]}, (low, low + tiles), []))[2].append(name)
+        entry = groups.setdefault(key, ({one: (0, 1), two: key[2], three: key[3]}, (low, low + tiles), set()))
+        entry[2].add(message["unit"])
     for part in PARTS:
-        groups[(part, 1, 0, 0)][2].append(("own", part))
+        groups[(part, 1, 0, 0)][2].add(("own", part))
     return list(groups.values())
 
 
-def schedule(found, joined):
+def schedule(found, units, joined):
     users = {}
     for name, message in found.items():
         for before in message["after"]:
             users.setdefault(before, []).append(name)
-    length = {name: count(message) * TILE_US for name, message in found.items()}
+    length = {name: count(message["region"], message["tiles"]) * TILE_US for name, message in found.items()}
     delay = {name: HOP_US + FAR_US * (message["far"] - 1) for name, message in found.items()}
     remaining = {}
 
     def path(name):
         if name not in remaining:
-            remaining[name] = length[name] + delay[name] + max([path(user) for user in users.get(name, [])] + [0.0])
+            after = [path(user) for user in users.get(found[name]["unit"], [])]
+            remaining[name] = length[name] + delay[name] + max(after + [0.0])
         return remaining[name]
 
     def lanes(link):
@@ -122,6 +137,7 @@
         return [((axis, 1), 1), ((axis, 3), 1)] if step == 2 else [(link, 1)]
 
     needs = {name: len(message["after"]) for name, message in found.items()}
+    flying = {unit: [len(names), 0.0] for unit, (_, _, names) in units.items()}
     cores = [set(names) for _, _, names in joined]
     arrivals = [(time, -1, ("own", part)) for part, time in READY.items()]
     heapq.heapify(arrivals)
@@ -154,8 +170,12 @@
             for lane, times in lanes(found[name]["link"]):
                 free[lane] = max(clock, free.get(lane, 0.0)) + length[name] * times
                 end = max(end, free[lane])
-            ticket += 1
-            heapq.heappush(arrivals, (end + delay[name], ticket, name))
+            flight = flying[found[name]["unit"]]
+            flight[0] -= 1
+            flight[1] = max(flight[1], end + delay[name])
+            if flight[0] == 0:
+                ticket += 1
+                heapq.heappush(arrivals, (flight[1], ticket, found[name]["unit"]))
             continue
         later = [until - LEAD_US + 1e-6 for until in backlog.values()]
         if arrivals:
@@ -190,7 +210,7 @@
 
 
 def exchange_kernel(
-    steps, found, joined,
+    steps, found, units, joined,
     lw_ref, base_ref, error_ref, momentum_ref, signs_ref, kept_ref,
     whole_ref, fresh_ref, dropped_ref,
     lw, base, error, momentum, signs, kept, part_sums, near, far, mine, outer,
@@ -271,10 +291,17 @@
         )
 
     def at(region, tiles):
-        every = slice(None)
-        spot_x = every if region["x"] is None else place_x(region["x"])
-        high, low = (every, every) if region["y"] is None else place_y(region["y"])
-        spot_z = every if region["z"] is None else place_z(region["z"])
+        def span(axis):
+            i, cuts = region[axis]
+            wide = SIZES[axis] // cuts
+            return pl.ds(i * wide, wide)
+
+        spot_x = span("x") if isinstance(region["x"], tuple) else place_x(region["x"])
+        spot_z = span("z") if isinstance(region["z"], tuple) else place_z(region["z"])
+        if isinstance(region["y"], tuple):
+            high, low = pl.ds(region["y"][0], 2 // region["y"][1]), slice(None)
+        else:
+            high, low = place_y(region["y"])
         return whole_ref.at[spot_z, spot_x, high, low, c, :, pl.ds(tiles[0] * LANES, (tiles[1] - tiles[0]) * LANES)]
 
     to_far = remote(part_sums.at[2 * (1 - p) + 1 - c], near.at[0], near_send.at[0], near_recv.at[0], other_core)
@@ -296,24 +323,28 @@
     to_mine.wait_recv()
     copies[8].wait()
 
-    names = {name: i for i, name in enumerate(name for name in found if name != OUTER)}
+    spots = {unit: i for i, unit in enumerate(unit for unit in units if unit != OUTER)}
     sums = {(part, stage): 3 * i + stage - 1 for i, part in enumerate(PARTS) for stage in (1, 2, 3)}
     mine_outer, their_outer = outer.at[2 * p + c], outer.at[2 * (1 - p) + c]
     outer_far = remote(mine_outer, mine_outer, outer_send.at[0], outer_recv.at[0], partner)
     outer_near = remote(mine_outer, mine_outer, outer_send.at[1], outer_recv.at[1], other_core)
     outer_last = remote(their_outer, their_outer, outer_send.at[2], outer_recv.at[2], other_core)
 
-    def moved(name, sender):
+    def send(name):
         message = found[name]
         axis, step = message["link"]
         region = dict(message["region"])
-        if sender:
-            region[axis] = region[axis] + step if axis == "z" else region[axis] ^ step
+        region[axis] = region[axis] + step if axis == "z" else region[axis] ^ step
         place = at(region, message["tiles"])
-        return remote(
+        remote(
             place, place, stage_send.at[sums[message["part"], message["stage"]]],
-            message_recv.at[names[name]], over(message["link"]),
-        )
+            message_recv.at[spots[message["unit"]]], over(message["link"]),
+        ).start()
+
+    def take(unit):
+        region, tiles, _ = units[unit]
+        place = at(region, tiles)
+        remote(place, place, core_send, message_recv.at[spots[unit]], other_core).wait_recv()
 
     def own(part):
         _, low, tiles = PARTS[part]
@@ -347,7 +378,7 @@
                 outer_far.start()
                 outer_near.start()
             else:
-                moved(what, True).start()
+                send(what)
             continue
         if what == OUTER:
             remote(their_outer, their_outer, outer_send.at[0], outer_recv.at[0], partner).wait_recv()
@@ -356,7 +387,7 @@
         if what[0] == "own":
             own(what[1])
         else:
-            moved(what, False).wait_recv()
+            take(what)
         for group, _, _ in waiting:
             group.discard(what)
         for _, region, tiles in [entry for entry in waiting if not entry[0]]:
@@ -366,10 +397,6 @@
     if outer_at + FINISH_AFTER >= len(steps):
         finish()
 
-    everything = whole_ref.at[:, :, :, :, 1 - c]
-    remote(everything, everything, core_send, core_recv, other_core).wait_recv()
-    everything = whole_ref.at[:, :, :, :, c]
-    remote(everything, everything, core_send, core_recv, other_core).wait_send()
     for part, (order, low, tiles) in PARTS.items():
         columns = pl.ds(low * LANES, tiles * LANES)
         for stage in (1, 2, 3):
@@ -386,6 +413,10 @@
     to_mine.wait_send()
     for copy in list(pieces.values()) + [outer_far, outer_near, outer_last]:
         copy.wait_send()
+    everything = whole_ref.at[:, :, :, :, c]
+    remote(everything, everything, core_send, core_recv, other_core).wait_send()
+    everything = whole_ref.at[:, :, :, :, 1 - c]
+    remote(everything, everything, core_send, core_recv, other_core).wait_recv()
 
 
 def store_kernel(whole_ref, fresh_ref, dropped_ref, base_out, error_out, momentum_out, sems):
@@ -413,12 +444,12 @@
     hbm = pl.BlockSpec(memory_space=pl.ANY)
     held = lambda array: pltpu.with_memory_space_constraint(array, pltpu.VMEM)
     stay = lambda array: pltpu.with_memory_space_constraint(array, pltpu.HBM)
-    found = messages()
+    found, units = messages()
     joined = forwards(found)
-    steps = schedule(found, joined)
+    steps = schedule(found, units, joined)
     dma = pltpu.SemaphoreType.DMA
     whole, fresh, dropped = pl.pallas_call(
-        functools.partial(exchange_kernel, steps, found, joined),
+        functools.partial(exchange_kernel, steps, found, units, joined),
         out_shape=(
             pltpu.VMEM((8, 4, 2, 2, 2, rows, QUARTER), jnp.bfloat16),
             pltpu.VMEM((rows, width), jnp.float32),
@@ -439,7 +470,7 @@
             pltpu.VMEM((rows, QUARTER), jnp.float32),
             pltpu.VMEM((4, rows, QUARTER), jnp.float32),
             dma((9,)), dma((2,)), dma((2,)), dma((3,)), dma((3,)), dma((3,)), dma((3,)),
-            dma((9,)), dma((len(found) - 1,)), dma, dma,
+            dma((9,)), dma((len(units) - 1,)), dma, dma,
         ],
         compiler_params=pltpu.CompilerParams(
             collective_id=0, has_side_effects=True, vmem_limit_bytes=16 << 20

time: 64.5 us -> 62.3 us (0.966)
  Pallas kernels: 63.8 us -> 61.5 us
    pallas_call x1, Pallas kernels: 57.4 us -> 55.1 us  [shards(): pl.pallas_call(functools.partial(exchange_kernel, steps, found, units, jo...]
where the time goes in v3:
time: 62.3 us; the launch traced here: 62.2 us
  Pallas kernels  61.5 us (99%)
  between operations  0.64 us (1%)
    pallas_call x1, Pallas kernels, shards(): pl.pallas_call(functools.partial(exchange_kernel, steps, found, units, jo...  55.1 us
    pallas_call x1, Pallas kernels, shards(): pl.pallas_call(store_kernel, out_shape=(jax.ShapeDtypeStruct((8, 4, 2, ro...  6.41 us

profile of v3, /device:TPU:1, one launch (start us, length us, event | category | flops | bytes accessed | tf_op | source)
XLA Modules:
  0.0 62.2 jit_solution(14185960092872990802)
XLA Ops:
  0.6 55.1 %exchange.1 = (bf16[8,4,2,2,2,16,2048]{6,5,4,3,2,1,0:T(8,128)(2,1)S(1)}, f32[16,8192]{1,0:T(8,128)S(1)}, f32[16,8192]{1,0:T(8,128)S(1)}) custom-call(bf16[1,16,8192]{2,1,0:T(8,128)(2,1)} %lw_ref.1, bf16[16,8192]{1,0:T(8,128)(2,1)} %base_ref.1, f32[1,16,8192]{2,1,0:T(8,128)} %error_ref.1, f32[16,8192]{1,0:T(8,128)} %momentum_ref.1, s32[64,128]{1,0:T(8,128)} %bitcast.2, ...), custom_call_target="tpu_custom_call" | custom-call | tf_op jit(solution)/shard_map/exchange/pallas_call | solution.py:451
  55.8 6.4 %store.1 = (bf16[8,4,2,16,8192]{4,3,2,1,0:T(8,128)(2,1)}, f32[1,16,8192]{2,1,0:T(8,128)}, f32[16,8192]{1,0:T(8,128)}) custom-call(bf16[8,4,2,2,2,16,2048]{6,5,4,3,2,1,0:T(8,128)(2,1)S(1)} %get-tuple-element.9.whole_ref, f32[16,8192]{1,0:T(8,128)S(1)} %get-tuple-element.10.fresh_ref, f32[16,8192]{1,0:T(8,128)S(1)} %get-tuple-element.11.dropped_ref), custom_call_target="tpu_custom_call" | custom-call | tf_op jit(solution)/shard_map/store/pallas_call | solution.py:484

commit v4 on v3

--- a/solution.py
+++ b/solution.py
@@ -12,12 +12,11 @@
 SIZES = {"x": 4, "y": 4, "z": 8}
 AXES = ("x", "y", "z")
 ROWS, QUARTER, LANES = 16, 2048, 128
-PARTS = {"A": ("xyz", 0, 4), "B": ("yzx", 4, 6), "C": ("zxy", 10, 6)}
-STRAIGHT = {("A", 1): (2,), ("B", 1): (2,), ("C", 1): (3,)}
-CUT = {("C", 3): 3}
-SINGLES = {"A": (1, 1), "B": (1, 1), "C": (1, 1)}
-READY = {"A": 0.0, "B": 0.9, "C": 1.6}
-TILE_US, HOP_US, FAR_US, OP_US, LEAD_US = 0.092, 3.1, 0.65, 0.01, 0.4
+PARTS = {"A": ("zxy", 0, 5), "B": ("zyx", 5, 6), "C": ("xyz", 11, 5)}
+STRAIGHT = {("A", 1): (2,), ("B", 1): (3,), ("C", 1): (2,)}
+CUT = {("A", 3): 3}
+SINGLES = {"A": (1, 1), "B": (1, 1), "C": (0, 1)}
+TILE_US, HOP_US, FAR_US, OP_US, LEAD_US = 0.092, 3.1, 0.65, 0.01, 0.8
 OUTER = ("outer",)
 OUTER_TILES = 32
 FINISH_AFTER = 40
@@ -139,7 +138,7 @@
     needs = {name: len(message["after"]) for name, message in found.items()}
     flying = {unit: [len(names), 0.0] for unit, (_, _, names) in units.items()}
     cores = [set(names) for _, _, names in joined]
-    arrivals = [(time, -1, ("own", part)) for part, time in READY.items()]
+    arrivals = [(2 * (low + tiles) * TILE_US, -1, ("own", part)) for part, (_, low, tiles) in PARTS.items()]
     heapq.heapify(arrivals)
     queues, free, steps = {}, {}, []
     clock, ticket = 0.0, 0
@@ -184,6 +183,32 @@
     return steps
 
 
+def share(found, units, steps):
+    at = {step: i for i, step in enumerate(steps)}
+    links = {}
+    for name, message in found.items():
+        if message["part"] is not None:
+            links.setdefault(message["link"], []).append((at["send", name], at["wait", message["unit"]]))
+
+    def known(unit, name):
+        axis, step = found[name]["link"]
+        back = (axis, -step) if axis == "z" else (axis, step)
+        over = at["wait", unit]
+        return any(sent > over and taken < at["send", name] for sent, taken in links.get(back, []))
+
+    spots, last = {}, []
+    rest = [unit for unit in units if unit != OUTER]
+    for unit in sorted(rest, key=lambda unit: min(at["send", name] for name in units[unit][2])):
+        free = [i for i, old in enumerate(last) if all(known(old, name) for name in units[unit][2])]
+        if free:
+            spots[unit] = max(free, key=lambda i: at["wait", last[i]])
+            last[spots[unit]] = unit
+        else:
+            spots[unit] = len(last)
+            last.append(unit)
+    return spots, len(last)
+
+
 def parity_table(rows, columns):
     i = lax.broadcasted_iota(jnp.int32, (rows, columns), 0)
     j = lax.broadcasted_iota(jnp.int32, (rows, columns), 1)
@@ -210,12 +235,12 @@
 
 
 def exchange_kernel(
-    steps, found, units, joined,
+    steps, found, units, joined, spots,
     lw_ref, base_ref, error_ref, momentum_ref, signs_ref, kept_ref,
     whole_ref, fresh_ref, dropped_ref,
     lw, base, error, momentum, signs, kept, part_sums, near, far, mine, outer,
     loads, near_send, near_recv, far_send, far_recv, outer_send, outer_recv,
-    stage_send, message_recv, core_send, core_recv,
+    all_send, message_recv, core_send, core_recv,
 ):
     rep, shard = lax.axis_index("rep"), lax.axis_index("shard")
     p, c = rep // 2, rep % 2
@@ -263,20 +288,22 @@
     table = parity_table(2 * LANES, LANES)
     scale = 1.0 / 64.0
 
-    def sketch(slot, b):
+    def kept_mask(b):
+        places = kept[pl.ds(b, 1), :]
+        tile_hot = lax.broadcasted_iota(jnp.int32, (tiles_of_block, places.shape[1]), 0) == jnp.right_shift(places, 7)
+        lane_hot = lax.broadcasted_iota(jnp.int32, (LANES, places.shape[1]), 0) == jnp.bitwise_and(places, LANES - 1)
+        return lax.dot_general(
+            tile_hot.astype(jnp.bfloat16), lane_hot.astype(jnp.bfloat16),
+            (((1,), (1,)), ((), ())), preferred_element_type=jnp.float32,
+        )[:, None, :]
+
+    def sketch(slot, b, mask):
         for copy in copies[2 + 3 * slot:5 + 3 * slot]:
             copy.wait()
         compensated = (base[slot].astype(jnp.float32) - lw[slot].astype(jnp.float32)) + error[slot]
         comp = jnp.stack([compensated[:, t * LANES:(t + 1) * LANES] for t in range(tiles_of_block)])
         rows = pl.ds(pl.multiple_of(b * tiles_of_block, tiles_of_block), tiles_of_block)
         turn = signs[rows, :].astype(jnp.float32)[:, None, :]
-        places = kept[pl.ds(b, 1), :]
-        tile_hot = lax.broadcasted_iota(jnp.int32, (tiles_of_block, places.shape[1]), 0) == jnp.right_shift(places, 7)
-        lane_hot = lax.broadcasted_iota(jnp.int32, (LANES, places.shape[1]), 0) == jnp.bitwise_and(places, LANES - 1)
-        mask = lax.dot_general(
-            tile_hot.astype(jnp.bfloat16), lane_hot.astype(jnp.bfloat16),
-            (((1,), (1,)), ((), ())), preferred_element_type=jnp.float32,
-        )[:, None, :]
         rotated = rotate(comp * turn, table) * scale
         back = rotate(jnp.where(mask > 0.5, rotated, 0.0), table) * (turn * scale)
         rest = comp - back
@@ -308,10 +335,11 @@
     to_mine = remote(part_sums.at[2 * p + 1 - c], near.at[1], near_send.at[1], near_recv.at[1], other_core)
     copies[0].wait()
     copies[1].wait()
-    sketch(0, 1 - p)
+    first_mask = kept_mask(1 - p)
+    sketch(0, 1 - p, first_mask)
     pl.semaphore_wait(barrier, len(peers))
     to_far.start()
-    sketch(1, p)
+    sketch(1, p, kept_mask(p))
     to_mine.start()
     to_far.wait_recv()
     pieces = {}
@@ -323,8 +351,6 @@
     to_mine.wait_recv()
     copies[8].wait()
 
-    spots = {unit: i for i, unit in enumerate(unit for unit in units if unit != OUTER)}
-    sums = {(part, stage): 3 * i + stage - 1 for i, part in enumerate(PARTS) for stage in (1, 2, 3)}
     mine_outer, their_outer = outer.at[2 * p + c], outer.at[2 * (1 - p) + c]
     outer_far = remote(mine_outer, mine_outer, outer_send.at[0], outer_recv.at[0], partner)
     outer_near = remote(mine_outer, mine_outer, outer_send.at[1], outer_recv.at[1], other_core)
@@ -337,8 +363,7 @@
         region[axis] = region[axis] + step if axis == "z" else region[axis] ^ step
         place = at(region, message["tiles"])
         remote(
-            place, place, stage_send.at[sums[message["part"], message["stage"]]],
-            message_recv.at[spots[message["unit"]]], over(message["link"]),
+            place, place, all_send, message_recv.at[spots[message["unit"]]], over(message["link"]),
         ).start()
 
     def take(unit):
@@ -408,7 +433,7 @@
                 place = whole_ref.at[
                     pl.ds(0, ends["z"]), pl.ds(0, ends["x"]), pl.ds(0, high), pl.ds(0, low_y), c, :, columns
                 ]
-                remote(place, place, stage_send.at[sums[part, stage]], core_recv, other_core).wait_send()
+                remote(place, place, all_send, core_recv, other_core).wait_send()
     to_far.wait_send()
     to_mine.wait_send()
     for copy in list(pieces.values()) + [outer_far, outer_near, outer_last]:
@@ -447,9 +472,10 @@
     found, units = messages()
     joined = forwards(found)
     steps = schedule(found, units, joined)
+    spots, number = share(found, units, steps)
     dma = pltpu.SemaphoreType.DMA
     whole, fresh, dropped = pl.pallas_call(
-        functools.partial(exchange_kernel, steps, found, units, joined),
+        functools.partial(exchange_kernel, steps, found, units, joined, spots),
         out_shape=(
             pltpu.VMEM((8, 4, 2, 2, 2, rows, QUARTER), jnp.bfloat16),
             pltpu.VMEM((rows, width), jnp.float32),
@@ -470,7 +496,7 @@
             pltpu.VMEM((rows, QUARTER), jnp.float32),
             pltpu.VMEM((4, rows, QUARTER), jnp.float32),
             dma((9,)), dma((2,)), dma((2,)), dma((3,)), dma((3,)), dma((3,)), dma((3,)),
-            dma((9,)), dma((len(units) - 1,)), dma, dma,
+            dma, dma((number,)), dma, dma,
         ],
         compiler_params=pltpu.CompilerParams(
             collective_id=0, has_side_effects=True, vmem_limit_bytes=16 << 20

time: 62.3 us -> 60.3 us (0.968)
  Pallas kernels: 61.5 us -> 59.6 us
    pallas_call x1, Pallas kernels: 55.1 us -> 53.2 us  [shards(): pl.pallas_call(functools.partial(exchange_kernel, steps, found, units, jo...]
where the time goes in v4:
time: 60.3 us; the launch traced here: 60.2 us
  Pallas kernels  59.6 us (99%)
  between operations  0.64 us (1%)
    pallas_call x1, Pallas kernels, shards(): pl.pallas_call(functools.partial(exchange_kernel, steps, found, units, jo...  53.2 us
    pallas_call x1, Pallas kernels, shards(): pl.pallas_call(store_kernel, out_shape=(jax.ShapeDtypeStruct((8, 4, 2, ro...  6.41 us

profile of v4, /device:TPU:1, one launch (start us, length us, event | category | flops | bytes accessed | tf_op | source)
XLA Modules:
  0.0 60.2 jit_solution(6246115890655328436)
XLA Ops:
  0.6 53.2 %exchange.1 = (bf16[8,4,2,2,2,16,2048]{6,5,4,3,2,1,0:T(8,128)(2,1)S(1)}, f32[16,8192]{1,0:T(8,128)S(1)}, f32[16,8192]{1,0:T(8,128)S(1)}) custom-call(bf16[1,16,8192]{2,1,0:T(8,128)(2,1)} %lw_ref.1, bf16[16,8192]{1,0:T(8,128)(2,1)} %base_ref.1, f32[1,16,8192]{2,1,0:T(8,128)} %error_ref.1, f32[16,8192]{1,0:T(8,128)} %momentum_ref.1, s32[64,128]{1,0:T(8,128)} %bitcast.2, ...), custom_call_target="tpu_custom_call" | custom-call | tf_op jit(solution)/shard_map/exchange/pallas_call | solution.py:477
  53.8 6.4 %store.1 = (bf16[8,4,2,16,8192]{4,3,2,1,0:T(8,128)(2,1)}, f32[1,16,8192]{2,1,0:T(8,128)}, f32[16,8192]{1,0:T(8,128)}) custom-call(bf16[8,4,2,2,2,16,2048]{6,5,4,3,2,1,0:T(8,128)(2,1)S(1)} %get-tuple-element.9.whole_ref, f32[16,8192]{1,0:T(8,128)S(1)} %get-tuple-element.10.fresh_ref, f32[16,8192]{1,0:T(8,128)S(1)} %get-tuple-element.11.dropped_ref), custom_call_target="tpu_custom_call" | custom-call | tf_op jit(solution)/shard_map/store/pallas_call | solution.py:510

commit v5 on v4

--- a/solution.py
+++ b/solution.py
@@ -239,7 +239,7 @@
     lw_ref, base_ref, error_ref, momentum_ref, signs_ref, kept_ref,
     whole_ref, fresh_ref, dropped_ref,
     lw, base, error, momentum, signs, kept, part_sums, near, far, mine, outer,
-    loads, near_send, near_recv, far_send, far_recv, outer_send, outer_recv,
+    loads, near_recv, far_recv, outer_recv,
     all_send, message_recv, core_send, core_recv,
 ):
     rep, shard = lax.axis_index("rep"), lax.axis_index("shard")
@@ -331,8 +331,8 @@
             high, low = place_y(region["y"])
         return whole_ref.at[spot_z, spot_x, high, low, c, :, pl.ds(tiles[0] * LANES, (tiles[1] - tiles[0]) * LANES)]
 
-    to_far = remote(part_sums.at[2 * (1 - p) + 1 - c], near.at[0], near_send.at[0], near_recv.at[0], other_core)
-    to_mine = remote(part_sums.at[2 * p + 1 - c], near.at[1], near_send.at[1], near_recv.at[1], other_core)
+    to_far = remote(part_sums.at[2 * (1 - p) + 1 - c], near.at[0], all_send, near_recv.at[0], other_core)
+    to_mine = remote(part_sums.at[2 * p + 1 - c], near.at[1], all_send, near_recv.at[1], other_core)
     copies[0].wait()
     copies[1].wait()
     first_mask = kept_mask(1 - p)
@@ -346,15 +346,15 @@
     for i, (part, (_, low, tiles)) in enumerate(PARTS.items()):
         columns = pl.ds(low * LANES, tiles * LANES)
         mine[:, columns] = part_sums[2 * (1 - p) + c, :, columns] + near[0, :, columns]
-        pieces[part] = remote(mine.at[:, columns], far.at[:, columns], far_send.at[i], far_recv.at[i], partner)
+        pieces[part] = remote(mine.at[:, columns], far.at[:, columns], all_send, far_recv.at[i], partner)
         pieces[part].start()
     to_mine.wait_recv()
     copies[8].wait()
 
     mine_outer, their_outer = outer.at[2 * p + c], outer.at[2 * (1 - p) + c]
-    outer_far = remote(mine_outer, mine_outer, outer_send.at[0], outer_recv.at[0], partner)
-    outer_near = remote(mine_outer, mine_outer, outer_send.at[1], outer_recv.at[1], other_core)
-    outer_last = remote(their_outer, their_outer, outer_send.at[2], outer_recv.at[2], other_core)
+    outer_far = remote(mine_outer, mine_outer, all_send, outer_recv.at[0], partner)
+    outer_near = remote(mine_outer, mine_outer, all_send, outer_recv.at[1], other_core)
+    outer_last = remote(their_outer, their_outer, all_send, outer_recv.at[2], other_core)
 
     def send(name):
         message = found[name]
@@ -386,9 +386,9 @@
 
     def finish():
         from_core = outer.at[2 * p + 1 - c]
-        remote(from_core, from_core, outer_send.at[1], outer_recv.at[1], other_core).wait_recv()
+        remote(from_core, from_core, all_send, outer_recv.at[1], other_core).wait_recv()
         from_core = outer.at[2 * (1 - p) + 1 - c]
-        remote(from_core, from_core, outer_send.at[2], outer_recv.at[2], other_core).wait_recv()
+        remote(from_core, from_core, all_send, outer_recv.at[2], other_core).wait_recv()
         for q in range(4):
             columns = pl.ds(q * QUARTER, QUARTER)
             fresh_ref[:, columns] = 0.9 * momentum[:, columns] + outer[q]
@@ -406,7 +406,7 @@
                 send(what)
             continue
         if what == OUTER:
-            remote(their_outer, their_outer, outer_send.at[0], outer_recv.at[0], partner).wait_recv()
+            remote(their_outer, their_outer, all_send, outer_recv.at[0], partner).wait_recv()
             outer_last.start()
             continue
         if what[0] == "own":
@@ -495,8 +495,7 @@
             pltpu.VMEM((rows, QUARTER), jnp.float32),
             pltpu.VMEM((rows, QUARTER), jnp.float32),
             pltpu.VMEM((4, rows, QUARTER), jnp.float32),
-            dma((9,)), dma((2,)), dma((2,)), dma((3,)), dma((3,)), dma((3,)), dma((3,)),
-            dma, dma((number,)), dma, dma,
+            dma((9,)), dma((2,)), dma((3,)), dma((3,)), dma, dma((number,)), dma, dma,
         ],
         compiler_params=pltpu.CompilerParams(
             collective_id=0, has_side_effects=True, vmem_limit_bytes=16 << 20

time: 60.3 us -> 60.3 us (level)
  no operation moved by 1% of the time
where the time goes in v5:
time: 60.3 us; the launch traced here: 60.1 us
  Pallas kernels  59.5 us (99%)
  between operations  0.64 us (1%)
    pallas_call x1, Pallas kernels, shards(): pl.pallas_call(functools.partial(exchange_kernel, steps, found, units, jo...  53.1 us
    pallas_call x1, Pallas kernels, shards(): pl.pallas_call(store_kernel, out_shape=(jax.ShapeDtypeStruct((8, 4, 2, ro...  6.41 us

profile of v5, /device:TPU:1, one launch (start us, length us, event | category | flops | bytes accessed | tf_op | source)
XLA Modules:
  0.0 60.1 jit_solution(14051959327818068924)
XLA Ops:
  0.6 53.1 %exchange.1 = (bf16[8,4,2,2,2,16,2048]{6,5,4,3,2,1,0:T(8,128)(2,1)S(1)}, f32[16,8192]{1,0:T(8,128)S(1)}, f32[16,8192]{1,0:T(8,128)S(1)}) custom-call(bf16[1,16,8192]{2,1,0:T(8,128)(2,1)} %lw_ref.1, bf16[16,8192]{1,0:T(8,128)(2,1)} %base_ref.1, f32[1,16,8192]{2,1,0:T(8,128)} %error_ref.1, f32[16,8192]{1,0:T(8,128)} %momentum_ref.1, s32[64,128]{1,0:T(8,128)} %bitcast.2, ...), custom_call_target="tpu_custom_call" | custom-call | tf_op jit(solution)/shard_map/exchange/pallas_call | solution.py:477
  53.7 6.4 %store.1 = (bf16[8,4,2,16,8192]{4,3,2,1,0:T(8,128)(2,1)}, f32[1,16,8192]{2,1,0:T(8,128)}, f32[16,8192]{1,0:T(8,128)}) custom-call(bf16[8,4,2,2,2,16,2048]{6,5,4,3,2,1,0:T(8,128)(2,1)S(1)} %get-tuple-element.9.whole_ref, f32[16,8192]{1,0:T(8,128)S(1)} %get-tuple-element.10.fresh_ref, f32[16,8192]{1,0:T(8,128)S(1)} %get-tuple-element.11.dropped_ref), custom_call_target="tpu_custom_call" | custom-call | tf_op jit(solution)/shard_map/store/pallas_call | solution.py:509

commit v6 on v5

--- a/solution.py
+++ b/solution.py
@@ -306,10 +306,13 @@
         turn = signs[rows, :].astype(jnp.float32)[:, None, :]
         rotated = rotate(comp * turn, table) * scale
         back = rotate(jnp.where(mask > 0.5, rotated, 0.0), table) * (turn * scale)
-        rest = comp - back
         half = tiles_of_block // 2
         for t in range(tiles_of_block):
             part_sums[2 * b + t // half, :, pl.ds((t % half) * LANES, LANES)] = back[t]
+        return comp - back
+
+    def keep_rest(b, rest):
+        for t in range(tiles_of_block):
             dropped_ref[:, pl.ds(pl.multiple_of(b * block + t * LANES, LANES), LANES)] = rest[t]
 
     def remote(source, target, send, recv, where):
@@ -331,23 +334,32 @@
             high, low = place_y(region["y"])
         return whole_ref.at[spot_z, spot_x, high, low, c, :, pl.ds(tiles[0] * LANES, (tiles[1] - tiles[0]) * LANES)]
 
-    to_far = remote(part_sums.at[2 * (1 - p) + 1 - c], near.at[0], all_send, near_recv.at[0], other_core)
-    to_mine = remote(part_sums.at[2 * p + 1 - c], near.at[1], all_send, near_recv.at[1], other_core)
+    first = next(iter(PARTS.values()))[2] * LANES
+    to_far = []
+    for i, columns in enumerate((pl.ds(0, first), pl.ds(first, QUARTER - first))):
+        to_far.append(remote(
+            part_sums.at[2 * (1 - p) + 1 - c, :, columns], near.at[0, :, columns], all_send, near_recv.at[i], other_core
+        ))
+    to_mine = remote(part_sums.at[2 * p + 1 - c], near.at[1], all_send, near_recv.at[2], other_core)
     copies[0].wait()
     copies[1].wait()
     first_mask = kept_mask(1 - p)
-    sketch(0, 1 - p, first_mask)
+    rest = sketch(0, 1 - p, first_mask)
     pl.semaphore_wait(barrier, len(peers))
-    to_far.start()
-    sketch(1, p, kept_mask(p))
+    for copy in to_far:
+        copy.start()
+    keep_rest(1 - p, rest)
+    rest = sketch(1, p, kept_mask(p))
     to_mine.start()
-    to_far.wait_recv()
     pieces = {}
     for i, (part, (_, low, tiles)) in enumerate(PARTS.items()):
         columns = pl.ds(low * LANES, tiles * LANES)
+        if i < 2:
+            to_far[i].wait_recv()
         mine[:, columns] = part_sums[2 * (1 - p) + c, :, columns] + near[0, :, columns]
         pieces[part] = remote(mine.at[:, columns], far.at[:, columns], all_send, far_recv.at[i], partner)
         pieces[part].start()
+    keep_rest(p, rest)
     to_mine.wait_recv()
     copies[8].wait()
 
@@ -434,9 +446,7 @@
                     pl.ds(0, ends["z"]), pl.ds(0, ends["x"]), pl.ds(0, high), pl.ds(0, low_y), c, :, columns
                 ]
                 remote(place, place, all_send, core_recv, other_core).wait_send()
-    to_far.wait_send()
-    to_mine.wait_send()
-    for copy in list(pieces.values()) + [outer_far, outer_near, outer_last]:
+    for copy in to_far + [to_mine] + list(pieces.values()) + [outer_far, outer_near, outer_last]:
         copy.wait_send()
     everything = whole_ref.at[:, :, :, :, c]
     remote(everything, everything, core_send, core_recv, other_core).wait_send()
@@ -495,7 +505,7 @@
             pltpu.VMEM((rows, QUARTER), jnp.float32),
             pltpu.VMEM((rows, QUARTER), jnp.float32),
             pltpu.VMEM((4, rows, QUARTER), jnp.float32),
-            dma((9,)), dma((2,)), dma((3,)), dma((3,)), dma, dma((number,)), dma, dma,
+            dma((9,)), dma((3,)), dma((3,)), dma((3,)), dma, dma((number,)), dma, dma,
         ],
         compiler_params=pltpu.CompilerParams(
             collective_id=0, has_side_effects=True, vmem_limit_bytes=16 << 20

time: 60.3 us -> 60.1 us (level)
  no operation moved by 1% of the time
where the time goes in v6:
time: 60.1 us; the launch traced here: 60 us
  Pallas kernels  59.3 us (99%)
  between operations  0.64 us (1%)
    pallas_call x1, Pallas kernels, shards(): pl.pallas_call(functools.partial(exchange_kernel, steps, found, units, jo...  52.9 us
    pallas_call x1, Pallas kernels, shards(): pl.pallas_call(store_kernel, out_shape=(jax.ShapeDtypeStruct((8, 4, 2, ro...  6.41 us

profile of v6, /device:TPU:1, one launch (start us, length us, event | category | flops | bytes accessed | tf_op | source)
XLA Modules:
  0.0 60.0 jit_solution(2046987544842068013)
XLA Ops:
  0.6 52.9 %exchange.1 = (bf16[8,4,2,2,2,16,2048]{6,5,4,3,2,1,0:T(8,128)(2,1)S(1)}, f32[16,8192]{1,0:T(8,128)S(1)}, f32[16,8192]{1,0:T(8,128)S(1)}) custom-call(bf16[1,16,8192]{2,1,0:T(8,128)(2,1)} %lw_ref.1, bf16[16,8192]{1,0:T(8,128)(2,1)} %base_ref.1, f32[1,16,8192]{2,1,0:T(8,128)} %error_ref.1, f32[16,8192]{1,0:T(8,128)} %momentum_ref.1, s32[64,128]{1,0:T(8,128)} %bitcast.2, ...), custom_call_target="tpu_custom_call" | custom-call | tf_op jit(solution)/shard_map/exchange/pallas_call | solution.py:487
  53.6 6.4 %store.1 = (bf16[8,4,2,16,8192]{4,3,2,1,0:T(8,128)(2,1)}, f32[1,16,8192]{2,1,0:T(8,128)}, f32[16,8192]{1,0:T(8,128)}) custom-call(bf16[8,4,2,2,2,16,2048]{6,5,4,3,2,1,0:T(8,128)(2,1)S(1)} %get-tuple-element.9.whole_ref, f32[16,8192]{1,0:T(8,128)S(1)} %get-tuple-element.10.fresh_ref, f32[16,8192]{1,0:T(8,128)S(1)} %get-tuple-element.11.dropped_ref), custom_call_target="tpu_custom_call" | custom-call | tf_op jit(solution)/shard_map/store/pallas_call | solution.py:519

commit v7 on v6

--- a/solution.py
+++ b/solution.py
@@ -277,7 +277,7 @@
             pltpu.make_async_copy(error_ref.at[0, :, columns], error.at[slot], loads.at[4 + 3 * slot]),
         ]
     copies.append(pltpu.make_async_copy(momentum_ref, momentum, loads.at[8]))
-    for copy in copies:
+    for copy in copies[:5]:
         copy.start()
 
     barrier = pltpu.get_barrier_semaphore()
@@ -300,6 +300,9 @@
     def sketch(slot, b, mask):
         for copy in copies[2 + 3 * slot:5 + 3 * slot]:
             copy.wait()
+        if slot == 0:
+            for copy in copies[5:]:
+                copy.start()
         compensated = (base[slot].astype(jnp.float32) - lw[slot].astype(jnp.float32)) + error[slot]
         comp = jnp.stack([compensated[:, t * LANES:(t + 1) * LANES] for t in range(tiles_of_block)])
         rows = pl.ds(pl.multiple_of(b * tiles_of_block, tiles_of_block), tiles_of_block)

time: 60.1 us -> 60.1 us (level)
  no operation moved by 1% of the time
where the time goes in v7:
time: 60.1 us; the launch traced here: 59.9 us
  Pallas kernels  59.3 us (99%)
  between operations  0.64 us (1%)
    pallas_call x1, Pallas kernels, shards(): pl.pallas_call(functools.partial(exchange_kernel, steps, found, units, jo...  52.9 us
    pallas_call x1, Pallas kernels, shards(): pl.pallas_call(store_kernel, out_shape=(jax.ShapeDtypeStruct((8, 4, 2, ro...  6.41 us

profile of v7, /device:TPU:1, one launch (start us, length us, event | category | flops | bytes accessed | tf_op | source)
XLA Modules:
  0.0 59.9 jit_solution(5199961513677477833)
XLA Ops:
  0.6 52.9 %exchange.1 = (bf16[8,4,2,2,2,16,2048]{6,5,4,3,2,1,0:T(8,128)(2,1)S(1)}, f32[16,8192]{1,0:T(8,128)S(1)}, f32[16,8192]{1,0:T(8,128)S(1)}) custom-call(bf16[1,16,8192]{2,1,0:T(8,128)(2,1)} %lw_ref.1, bf16[16,8192]{1,0:T(8,128)(2,1)} %base_ref.1, f32[1,16,8192]{2,1,0:T(8,128)} %error_ref.1, f32[16,8192]{1,0:T(8,128)} %momentum_ref.1, s32[64,128]{1,0:T(8,128)} %bitcast.2, ...), custom_call_target="tpu_custom_call" | custom-call | tf_op jit(solution)/shard_map/exchange/pallas_call | solution.py:490
  53.5 6.4 %store.1 = (bf16[8,4,2,16,8192]{4,3,2,1,0:T(8,128)(2,1)}, f32[1,16,8192]{2,1,0:T(8,128)}, f32[16,8192]{1,0:T(8,128)}) custom-call(bf16[8,4,2,2,2,16,2048]{6,5,4,3,2,1,0:T(8,128)(2,1)S(1)} %get-tuple-element.9.whole_ref, f32[16,8192]{1,0:T(8,128)S(1)} %get-tuple-element.10.fresh_ref, f32[16,8192]{1,0:T(8,128)S(1)} %get-tuple-element.11.dropped_ref), custom_call_target="tpu_custom_call" | custom-call | tf_op jit(solution)/shard_map/store/pallas_call | solution.py:522
